TPU v7x, 32 devices: a whole 2x2x4 slice. The times are simulated.
32 devices in a mesh: rad: 4 (over z), azi: 8 (over y, x, core).
Axes of the slice: x: 2, y: 2, z: 4, core: 2. Of those that a mesh axis runs over, the one named last changes fastest.
Arguments:
- fields: float32 [5, 1, 512, 512], P(None, None, 'azi', 'rad'), may hold values from -2 to 2, as said below
- shifts: int32 [3, 512], P(None, 'rad'), may hold values from 0 to 192, as said below
Outputs:
- advanced: float32 [5, 1, 512, 512], P(None, None, 'azi', 'rad')
Inputs may be any that keep to these rules, and one draw needn't show every extreme that they name: `fields`: every field component lies within -2 to 2; temperature within 0.5 to 1.5. `shifts`: each step has a row with shift 192 and a row with shift 0.
All inputs are finite; a program needn't handle non-finite values.
Results may differ from a plain program's by a relative error of at most 0.00002.
Values sent between devices are 32-bit elements; how exact they have to be, the bound alone decides.
A program may use at most 64 MiB of HBM per device.

v0:
```python
import jax
import jax.numpy as jnp
from jax import lax
from jax.sharding import PartitionSpec as P

STEPS = 3
SMAX = 192


courant = 0.2
viscous = 0.1


def passed_along(value, axis, steps):
    count = lax.axis_size(axis)
    pairs = [(source, (source + steps) % count) for source in range(count)]
    return lax.ppermute(value, axis, pairs)


def padded_2(value, sides, width, wrap):
    for axis, dim in sides:
        count, length = (lax.axis_size(axis), value.shape[dim])
        up = [(i, (i + 1) % count) for i in range(count if wrap else count - 1)]
        down = [(j, i) for i, j in up]
        last = lax.slice_in_dim(value, length - width, length, axis=dim)
        initial = lax.slice_in_dim(value, 0, width, axis=dim)
        before = lax.ppermute(last, axis, up)
        after = lax.ppermute(initial, axis, down)
        value = jnp.concatenate([before, value, after], axis=dim)
    return value


def update(padded, inverse):
    centre = padded[:, :, 1:-1, 1:-1]
    inner = padded[:, :, 1:-1, :-2]
    outer = padded[:, :, 1:-1, 2:]
    behind = padded[:, :, :-2, 1:-1]
    ahead = padded[:, :, 2:, 1:-1]
    polar_pad = jnp.concatenate([centre, centre, centre], axis=1)
    polar_sum = polar_pad[:, 2:] + polar_pad[:, :-2]
    radial_vel = centre[1]
    azim_vel = centre[2]
    advect = courant * (
        jnp.maximum(radial_vel, 0.0) * (centre - inner)
        + jnp.minimum(radial_vel, 0.0) * (outer - centre)
        + inverse
        * (
            jnp.maximum(azim_vel, 0.0) * (centre - behind)
            + jnp.minimum(azim_vel, 0.0) * (ahead - centre)
        )
    )
    laplace = (
        outer
        + inner
        - 2.0 * centre
        + inverse * inverse * (ahead + behind - 2.0 * centre)
        + (polar_sum - 2.0 * centre)
    )
    radial_diff = (outer - inner) * 0.5
    azim_diff = (ahead - behind) * 0.5
    diverge = radial_diff[1] + inverse * azim_diff[2]
    log_rho = centre[0]
    temper = centre[4]
    new_log = log_rho - advect[0] - courant * diverge
    new_radial = (
        radial_vel
        - advect[1]
        - courant * (temper * radial_diff[0] + radial_diff[4])
        + 0.5 * courant * inverse * azim_vel * azim_vel
        + viscous * laplace[1]
    )
    new_azim = (
        azim_vel
        - advect[2]
        - courant * inverse * (temper * azim_diff[0] + azim_diff[4])
        - 0.5 * courant * inverse * radial_vel * azim_vel
        + viscous * laplace[2]
    )
    new_polar = centre[3] - advect[3] + viscous * laplace[3]
    new_temper = temper - advect[4] - courant * 0.4 * temper * diverge + viscous * laplace[4]
    return jnp.stack([new_log, new_radial, new_azim, new_polar, new_temper])


def rotate_pieces(fields, offsets):
    width = fields.shape[2]
    count = (SMAX + width - 1) // width
    pieces = [fields]
    for blocks in range(1, count + 1):
        pieces.append(passed_along(fields, "azi", blocks))
    extended = jnp.concatenate(pieces[::-1], axis=2)
    nbits = SMAX.bit_length()
    reach = (1 << nbits) - 1
    anchor = count * width
    front = jnp.zeros(fields.shape[:2] + (reach - anchor,) + fields.shape[3:], fields.dtype)
    window = jnp.concatenate([front, extended], axis=2)
    for bit in range(nbits):
        amount = 1 << bit
        length = window.shape[2] - amount
        chosen = offsets // amount % 2 == 1
        window = jnp.where(
            chosen[None, None, None, :], window[:, :, :length], window[:, :, amount:]
        )
    return window


def local(fields, shifts):
    rows = fields.shape[3]
    total_rows = rows * lax.axis_size("rad")
    row_index = lax.axis_index("rad") * rows + jnp.arange(rows, dtype=jnp.int32)
    radius = 1.0 + (row_index.astype(jnp.float32) + 0.5) / jnp.float32(total_rows)
    inverse = 1.0 / radius
    for step in range(STEPS):
        radial_pad = padded_2(fields, (("rad", 3),), 1, False)
        padded = padded_2(radial_pad, (("azi", 2),), 1, True)
        fields = update(padded, inverse)
        fields = rotate_pieces(fields, shifts[step])
    return fields


def solution(mesh):
    placed = (P(None, None, "azi", "rad"), P(None, "rad"))
    return jax.shard_map(
        local, mesh=mesh, in_specs=placed, out_specs=P(None, None, "azi", "rad"), check_vma=False
    )
```

profile of v0, /device:TPU:0, one launch (start us, length us, event | category | flops | bytes accessed | tf_op | source)
XLA Modules:
  0.0 89.8 jit_solution(13413156783729175813)
XLA Ops:
  0.0 1.2 %fusion.105 = (f32[5,1,64,1]{3,2,1,0:T(8,128)S(1)}, f32[5,1,64,1]{3,2,1,0:T(8,128)S(1)}) fusion(f32[5,1,64,128]{3,2,1,0:T(8,128)} %param.2), kind=kLoop, calls=%fused_computation.375 | loop fusion | bytes 5120 | tf_op jit(solution)/shard_map/slice | solution.py:26
  1.2 4.9 %collective-permute-start = (f32[5,1,64,1]{3,2,1,0:T(8,128)S(1)}, f32[5,1,64,1]{3,2,1,0:T(8,128)S(1)}, u32[]{:S(2)}, u32[]{:S(2)}) collective-permute-start(f32[5,1,64,1]{3,2,1,0:T(8,128)S(1)} %get-tuple-element.30), channel_id=1, source_target_pairs={{0,8},{8,16},{16,24},{1,9},{9,17},{17,25},{2,10},{10,18},{18,26},{... | collective-permute-start | bytes 3848 | tf_op jit(solution)/shard_map/ppermute | solution.py:27
  6.1 1.3 %collective-permute-start.1 = (f32[5,1,64,1]{3,2,1,0:T(8,128)S(1)}, f32[5,1,64,1]{3,2,1,0:T(8,128)S(1)}, u32[]{:S(2)}, u32[]{:S(2)}) collective-permute-start(f32[5,1,64,1]{3,2,1,0:T(8,128)S(1)} %get-tuple-element.29), channel_id=1, source_target_pairs={{8,0},{16,8},{24,16},{9,1},{17,9},{25,17},{10,2},{18,10},{26,18},{... | collective-permute-start | bytes 3848 | tf_op jit(solution)/shard_map/ppermute | solution.py:28
  7.5 0.7 copy-done.1
  8.1 0.1 fusion.54
  8.2 1.3 %collective-permute-done = f32[5,1,64,1]{3,2,1,0:T(8,128)S(1)} collective-permute-done((f32[5,1,64,1]{3,2,1,0:T(8,128)S(1)}, f32[5,1,64,1]{3,2,1,0:T(8,128)S(1)}, u32[]{:S(2)}, u32[]{:S(2)}) %collective-permute-start) | collective-permute-done | bytes 1312 | tf_op jit(solution)/shard_map/ppermute | solution.py:27
  9.5 4.1 %collective-permute-done.1 = f32[5,1,64,1]{3,2,1,0:T(8,128)S(1)} collective-permute-done((f32[5,1,64,1]{3,2,1,0:T(8,128)S(1)}, f32[5,1,64,1]{3,2,1,0:T(8,128)S(1)}, u32[]{:S(2)}, u32[]{:S(2)}) %collective-permute-start.1) | collective-permute-done | bytes 1312 | tf_op jit(solution)/shard_map/ppermute | solution.py:28
  13.7 0.1 pad_maximum_fusion.30
  13.8 0.1 collective-permute-start.2
  13.8 2.6 %collective-permute-start.3 = (f32[5,1,1,130]{3,2,1,0:T(1,128)S(1)}, f32[5,1,1,130]{3,2,1,0:T(1,128)S(1)}, u32[]{:S(2)}, u32[]{:S(2)}) collective-permute-start(f32[5,1,1,130]{3,2,1,0:T(1,128)S(1)} %get-tuple-element.15), channel_id=1, source_target_pairs={{1,0},{2,1},{3,2},{4,3},{5,4},{6,5},{7,6},{0,7},{9,8},{10,9},{11,1... | collective-permute-start | bytes 7808 | tf_op jit(solution)/shard_map/ppermute | solution.py:28
  16.5 1.3 %collective-permute-done.2 = f32[5,1,1,130]{3,2,1,0:T(1,128)S(1)} collective-permute-done((f32[5,1,1,130]{3,2,1,0:T(1,128)S(1)}, f32[5,1,1,130]{3,2,1,0:T(1,128)S(1)}, u32[]{:S(2)}, u32[]{:S(2)}) %collective-permute-start.2) | collective-permute-done | bytes 2632 | tf_op jit(solution)/shard_map/ppermute | solution.py:27
  17.8 0.2 subtract_multiply_fusion.4
  18.0 0.3 subtract_add_fusion.2
  18.3 0.3 add_multiply_fusion.2
  18.7 2.7 %collective-permute-start.4 = (f32[5,1,64,128]{3,2,1,0:T(8,128)S(1)}, f32[5,1,64,128]{3,2,1,0:T(8,128)S(1)}, u32[]{:S(2)}, u32[]{:S(2)}) collective-permute-start(f32[5,1,64,128]{3,2,1,0:T(8,128)S(1)} %fusion.40), channel_id=1, source_target_pairs={{0,3},{1,4},{2,5},{3,6},{4,7},{5,0},{6,1},{7,2},{8,11},{9,12},{10,... | collective-permute-start | bytes 491528 | tf_op jit(solution)/shard_map/ppermute | solution.py:17
  21.4 0.6 collective-permute-start.5
  22.0 3.9 %collective-permute-done.4 = f32[5,1,64,128]{3,2,1,0:T(8,128)S(1)} collective-permute-done((f32[5,1,64,128]{3,2,1,0:T(8,128)S(1)}, f32[5,1,64,128]{3,2,1,0:T(8,128)S(1)}, u32[]{:S(2)}, u32[]{:S(2)}) %collective-permute-start.4) | collective-permute-done | bytes 163872 | tf_op jit(solution)/shard_map/ppermute | solution.py:17
  25.9 4.3 %collective-permute-done.5 = f32[5,1,64,128]{3,2,1,0:T(8,128)S(1)} collective-permute-done((f32[5,1,64,128]{3,2,1,0:T(8,128)S(1)}, f32[5,1,64,128]{3,2,1,0:T(8,128)S(1)}, u32[]{:S(2)}, u32[]{:S(2)}) %collective-permute-start.5) | collective-permute-done | bytes 163872 | tf_op jit(solution)/shard_map/ppermute | solution.py:17
  30.3 0.3 collective-permute-done.6
  30.6 0.8 concatenate.62
  31.4 0.1 slice_select_fusion.5
  31.5 0.1 slice_select_fusion.4
  31.6 0.1 slice_select_fusion.8
  32.0 0.1 fusion.104
  32.1 3.5 %collective-permute-start.7 = (f32[5,1,64,1]{3,2,1,0:T(8,128)S(1)}, f32[5,1,64,1]{3,2,1,0:T(8,128)S(1)}, u32[]{:S(2)}, u32[]{:S(2)}) collective-permute-start(f32[5,1,64,1]{3,2,1,0:T(8,128)S(1)} %get-tuple-element.24), channel_id=1, source_target_pairs={{0,8},{8,16},{16,24},{1,9},{9,17},{17,25},{2,10},{10,18},{18,26},{... | collective-permute-start | bytes 3848 | tf_op jit(solution)/shard_map/ppermute | solution.py:27
  35.6 1.3 %collective-permute-start.8 = (f32[5,1,64,1]{3,2,1,0:T(8,128)S(1)}, f32[5,1,64,1]{3,2,1,0:T(8,128)S(1)}, u32[]{:S(2)}, u32[]{:S(2)}) collective-permute-start(f32[5,1,64,1]{3,2,1,0:T(8,128)S(1)} %get-tuple-element.23), channel_id=1, source_target_pairs={{8,0},{16,8},{24,16},{9,1},{17,9},{25,17},{10,2},{18,10},{26,18},{... | collective-permute-start | bytes 3848 | tf_op jit(solution)/shard_map/ppermute | solution.py:28
  36.9 1.5 %collective-permute-done.7 = f32[5,1,64,1]{3,2,1,0:T(8,128)S(1)} collective-permute-done((f32[5,1,64,1]{3,2,1,0:T(8,128)S(1)}, f32[5,1,64,1]{3,2,1,0:T(8,128)S(1)}, u32[]{:S(2)}, u32[]{:S(2)}) %collective-permute-start.7) | collective-permute-done | bytes 1312 | tf_op jit(solution)/shard_map/ppermute | solution.py:27
  38.4 4.4 %collective-permute-done.8 = f32[5,1,64,1]{3,2,1,0:T(8,128)S(1)} collective-permute-done((f32[5,1,64,1]{3,2,1,0:T(8,128)S(1)}, f32[5,1,64,1]{3,2,1,0:T(8,128)S(1)}, u32[]{:S(2)}, u32[]{:S(2)}) %collective-permute-start.8) | collective-permute-done | bytes 1312 | tf_op jit(solution)/shard_map/ppermute | solution.py:28
  42.8 0.1 pad_maximum_fusion.27
  42.9 0.1 collective-permute-start.10
  42.9 0.5 collective-permute-start.9
  43.5 0.8 collective-permute-done.10
  44.3 2.7 %collective-permute-done.9 = f32[5,1,1,130]{3,2,1,0:T(1,128)S(1)} collective-permute-done((f32[5,1,1,130]{3,2,1,0:T(1,128)S(1)}, f32[5,1,1,130]{3,2,1,0:T(1,128)S(1)}, u32[]{:S(2)}, u32[]{:S(2)}) %collective-permute-start.9) | collective-permute-done | bytes 2632 | tf_op jit(solution)/shard_map/ppermute | solution.py:27
  46.9 0.3 subtract_add_fusion.1
  47.2 0.2 subtract_multiply_fusion.2
  47.4 0.3 add_multiply_fusion.1
  47.8 0.1 collective-permute-start.11
  47.9 0.2 collective-permute-start.12
  48.1 1.4 %collective-permute-start.13 = (f32[5,1,64,128]{3,2,1,0:T(8,128)S(1)}, f32[5,1,64,128]{3,2,1,0:T(8,128)S(1)}, u32[]{:S(2)}, u32[]{:S(2)}) collective-permute-start(f32[5,1,64,128]{3,2,1,0:T(8,128)S(1)} %fusion.25), channel_id=1, source_target_pairs={{0,1},{1,2},{2,3},{3,4},{4,5},{5,6},{6,7},{7,0},{8,9},{9,10},{10,1... | collective-permute-start | bytes 491528 | tf_op jit(solution)/shard_map/ppermute | solution.py:17
  49.5 9.6 %collective-permute-done.11 = f32[5,1,64,128]{3,2,1,0:T(8,128)S(1)} collective-permute-done((f32[5,1,64,128]{3,2,1,0:T(8,128)S(1)}, f32[5,1,64,128]{3,2,1,0:T(8,128)S(1)}, u32[]{:S(2)}, u32[]{:S(2)}) %collective-permute-start.11) | collective-permute-done | bytes 163872 | tf_op jit(solution)/shard_map/ppermute | solution.py:17
  59.1 0.8 concatenate.68
  59.9 0.1 slice_select_fusion.3
  60.0 0.1 slice_select_fusion.2
  60.1 0.1 slice_select_fusion.7
  60.4 0.1 fusion.103
  60.6 3.5 %collective-permute-start.14 = (f32[5,1,64,1]{3,2,1,0:T(8,128)S(1)}, f32[5,1,64,1]{3,2,1,0:T(8,128)S(1)}, u32[]{:S(2)}, u32[]{:S(2)}) collective-permute-start(f32[5,1,64,1]{3,2,1,0:T(8,128)S(1)} %get-tuple-element.18), channel_id=1, source_target_pairs={{0,8},{8,16},{16,24},{1,9},{9,17},{17,25},{2,10},{10,18},{18,26},{... | collective-permute-start | bytes 3848 | tf_op jit(solution)/shard_map/ppermute | solution.py:27
  64.0 1.3 %collective-permute-start.15 = (f32[5,1,64,1]{3,2,1,0:T(8,128)S(1)}, f32[5,1,64,1]{3,2,1,0:T(8,128)S(1)}, u32[]{:S(2)}, u32[]{:S(2)}) collective-permute-start(f32[5,1,64,1]{3,2,1,0:T(8,128)S(1)} %get-tuple-element.17), channel_id=1, source_target_pairs={{8,0},{16,8},{24,16},{9,1},{17,9},{25,17},{10,2},{18,10},{26,18},{... | collective-permute-start | bytes 3848 | tf_op jit(solution)/shard_map/ppermute | solution.py:28
  65.3 1.5 %collective-permute-done.14 = f32[5,1,64,1]{3,2,1,0:T(8,128)S(1)} collective-permute-done((f32[5,1,64,1]{3,2,1,0:T(8,128)S(1)}, f32[5,1,64,1]{3,2,1,0:T(8,128)S(1)}, u32[]{:S(2)}, u32[]{:S(2)}) %collective-permute-start.14) | collective-permute-done | bytes 1312 | tf_op jit(solution)/shard_map/ppermute | solution.py:27
  66.9 4.4 %collective-permute-done.15 = f32[5,1,64,1]{3,2,1,0:T(8,128)S(1)} collective-permute-done((f32[5,1,64,1]{3,2,1,0:T(8,128)S(1)}, f32[5,1,64,1]{3,2,1,0:T(8,128)S(1)}, u32[]{:S(2)}, u32[]{:S(2)}) %collective-permute-start.15) | collective-permute-done | bytes 1312 | tf_op jit(solution)/shard_map/ppermute | solution.py:28
  71.3 0.1 pad_maximum_fusion.24
  71.4 0.1 collective-permute-start.16
  71.4 2.6 %collective-permute-start.17 = (f32[5,1,1,130]{3,2,1,0:T(1,128)S(1)}, f32[5,1,1,130]{3,2,1,0:T(1,128)S(1)}, u32[]{:S(2)}, u32[]{:S(2)}) collective-permute-start(f32[5,1,1,130]{3,2,1,0:T(1,128)S(1)} %get-tuple-element.7), channel_id=1, source_target_pairs={{1,0},{2,1},{3,2},{4,3},{5,4},{6,5},{7,6},{0,7},{9,8},{10,9},{11,1... | collective-permute-start | bytes 7808 | tf_op jit(solution)/shard_map/ppermute | solution.py:28
  74.1 1.3 %collective-permute-done.16 = f32[5,1,1,130]{3,2,1,0:T(1,128)S(1)} collective-permute-done((f32[5,1,1,130]{3,2,1,0:T(1,128)S(1)}, f32[5,1,1,130]{3,2,1,0:T(1,128)S(1)}, u32[]{:S(2)}, u32[]{:S(2)}) %collective-permute-start.16) | collective-permute-done | bytes 2632 | tf_op jit(solution)/shard_map/ppermute | solution.py:27
  75.4 0.3 subtract_add_fusion
  75.7 0.2 subtract_multiply_fusion
  75.9 0.3 add_multiply_fusion
  76.3 2.0 %collective-permute-start.18 = (f32[5,1,64,128]{3,2,1,0:T(8,128)S(1)}, f32[5,1,64,128]{3,2,1,0:T(8,128)S(1)}, u32[]{:S(2)}, u32[]{:S(2)}) collective-permute-start(f32[5,1,64,128]{3,2,1,0:T(8,128)S(1)} %fusion.10), channel_id=1, source_target_pairs={{0,3},{1,4},{2,5},{3,6},{4,7},{5,0},{6,1},{7,2},{8,11},{9,12},{10,... | collective-permute-start | bytes 491528 | tf_op jit(solution)/shard_map/ppermute | solution.py:17
  78.3 0.2 collective-permute-start.20
  78.5 9.3 %collective-permute-done.18 = f32[5,1,64,128]{3,2,1,0:T(8,128)S(1)} collective-permute-done((f32[5,1,64,128]{3,2,1,0:T(8,128)S(1)}, f32[5,1,64,128]{3,2,1,0:T(8,128)S(1)}, u32[]{:S(2)}, u32[]{:S(2)}) %collective-permute-start.18) | collective-permute-done | bytes 163872 | tf_op jit(solution)/shard_map/ppermute | solution.py:17
  87.8 0.8 concatenate.74
  88.6 0.1 slice_select_fusion.1
  88.7 0.1 slice_select_fusion
  88.8 0.1 slice_select_fusion.6
  89.1 0.7 slice_select_fusion.21
  (47 shorter events, 1.1 us)
Async XLA Ops:
  0.0 7.4 %copy-start = (f32[5,1,64,128]{3,2,1,0:T(8,128)S(1)}, f32[5,1,64,128]{3,2,1,0:T(8,128)}, u32[]{:S(2)}) copy-start(f32[5,1,64,128]{3,2,1,0:T(8,128)} %param.2) | copy-start | bytes 491524
  1.2 8.4 %collective-permute-start = (f32[5,1,64,1]{3,2,1,0:T(8,128)S(1)}, f32[5,1,64,1]{3,2,1,0:T(8,128)S(1)}, u32[]{:S(2)}, u32[]{:S(2)}) collective-permute-start(f32[5,1,64,1]{3,2,1,0:T(8,128)S(1)} %get-tuple-element.30), channel_id=1, source_target_pairs={{0,8},{8,16},{16,24},{1,9},{9,17},{17,25},{2,10},{10,18},{18,26},{... | collective-permute-start | bytes 3848 | tf_op jit(solution)/shard_map/ppermute | solution.py:27
  6.1 7.6 %collective-permute-start.1 = (f32[5,1,64,1]{3,2,1,0:T(8,128)S(1)}, f32[5,1,64,1]{3,2,1,0:T(8,128)S(1)}, u32[]{:S(2)}, u32[]{:S(2)}) collective-permute-start(f32[5,1,64,1]{3,2,1,0:T(8,128)S(1)} %get-tuple-element.29), channel_id=1, source_target_pairs={{8,0},{16,8},{24,16},{9,1},{17,9},{25,17},{10,2},{18,10},{26,18},{... | collective-permute-start | bytes 3848 | tf_op jit(solution)/shard_map/ppermute | solution.py:28
  7.5 0.7 copy-start.1
  13.8 4.0 %collective-permute-start.2 = (f32[5,1,1,130]{3,2,1,0:T(1,128)S(1)}, f32[5,1,1,130]{3,2,1,0:T(1,128)S(1)}, u32[]{:S(2)}, u32[]{:S(2)}) collective-permute-start(f32[5,1,1,130]{3,2,1,0:T(1,128)S(1)} %get-tuple-element.16), channel_id=1, source_target_pairs={{0,1},{1,2},{2,3},{3,4},{4,5},{5,6},{6,7},{7,0},{8,9},{9,10},{10,1... | collective-permute-start | bytes 7808 | tf_op jit(solution)/shard_map/ppermute | solution.py:27
  13.8 4.0 %collective-permute-start.3 = (f32[5,1,1,130]{3,2,1,0:T(1,128)S(1)}, f32[5,1,1,130]{3,2,1,0:T(1,128)S(1)}, u32[]{:S(2)}, u32[]{:S(2)}) collective-permute-start(f32[5,1,1,130]{3,2,1,0:T(1,128)S(1)} %get-tuple-element.15), channel_id=1, source_target_pairs={{1,0},{2,1},{3,2},{4,3},{5,4},{6,5},{7,6},{0,7},{9,8},{10,9},{11,1... | collective-permute-start | bytes 7808 | tf_op jit(solution)/shard_map/ppermute | solution.py:28
  18.7 7.2 %collective-permute-start.4 = (f32[5,1,64,128]{3,2,1,0:T(8,128)S(1)}, f32[5,1,64,128]{3,2,1,0:T(8,128)S(1)}, u32[]{:S(2)}, u32[]{:S(2)}) collective-permute-start(f32[5,1,64,128]{3,2,1,0:T(8,128)S(1)} %fusion.40), channel_id=1, source_target_pairs={{0,3},{1,4},{2,5},{3,6},{4,7},{5,0},{6,1},{7,2},{8,11},{9,12},{10,... | collective-permute-start | bytes 491528 | tf_op jit(solution)/shard_map/ppermute | solution.py:17
  21.4 8.8 %collective-permute-start.5 = (f32[5,1,64,128]{3,2,1,0:T(8,128)S(1)}, f32[5,1,64,128]{3,2,1,0:T(8,128)S(1)}, u32[]{:S(2)}, u32[]{:S(2)}) collective-permute-start(f32[5,1,64,128]{3,2,1,0:T(8,128)S(1)} %fusion.40), channel_id=1, source_target_pairs={{0,2},{1,3},{2,4},{3,5},{4,6},{5,7},{6,0},{7,1},{8,10},{9,11},{10,... | collective-permute-start | bytes 491528 | tf_op jit(solution)/shard_map/ppermute | solution.py:17
  22.0 8.6 %collective-permute-start.6 = (f32[5,1,64,128]{3,2,1,0:T(8,128)S(1)}, f32[5,1,64,128]{3,2,1,0:T(8,128)S(1)}, u32[]{:S(2)}, u32[]{:S(2)}) collective-permute-start(f32[5,1,64,128]{3,2,1,0:T(8,128)S(1)} %fusion.40), channel_id=1, source_target_pairs={{0,1},{1,2},{2,3},{3,4},{4,5},{5,6},{6,7},{7,0},{8,9},{9,10},{10,1... | collective-permute-start | bytes 491528 | tf_op jit(solution)/shard_map/ppermute | solution.py:17
  32.1 6.3 %collective-permute-start.7 = (f32[5,1,64,1]{3,2,1,0:T(8,128)S(1)}, f32[5,1,64,1]{3,2,1,0:T(8,128)S(1)}, u32[]{:S(2)}, u32[]{:S(2)}) collective-permute-start(f32[5,1,64,1]{3,2,1,0:T(8,128)S(1)} %get-tuple-element.24), channel_id=1, source_target_pairs={{0,8},{8,16},{16,24},{1,9},{9,17},{17,25},{2,10},{10,18},{18,26},{... | collective-permute-start | bytes 3848 | tf_op jit(solution)/shard_map/ppermute | solution.py:27
  35.6 7.2 %collective-permute-start.8 = (f32[5,1,64,1]{3,2,1,0:T(8,128)S(1)}, f32[5,1,64,1]{3,2,1,0:T(8,128)S(1)}, u32[]{:S(2)}, u32[]{:S(2)}) collective-permute-start(f32[5,1,64,1]{3,2,1,0:T(8,128)S(1)} %get-tuple-element.23), channel_id=1, source_target_pairs={{8,0},{16,8},{24,16},{9,1},{17,9},{25,17},{10,2},{18,10},{26,18},{... | collective-permute-start | bytes 3848 | tf_op jit(solution)/shard_map/ppermute | solution.py:28
  42.9 1.4 %collective-permute-start.10 = (f32[5,1,1,130]{3,2,1,0:T(1,128)S(1)}, f32[5,1,1,130]{3,2,1,0:T(1,128)S(1)}, u32[]{:S(2)}, u32[]{:S(2)}) collective-permute-start(f32[5,1,1,130]{3,2,1,0:T(1,128)S(1)} %get-tuple-element.11), channel_id=1, source_target_pairs={{1,0},{2,1},{3,2},{4,3},{5,4},{6,5},{7,6},{0,7},{9,8},{10,9},{11,1... | collective-permute-start | bytes 7808 | tf_op jit(solution)/shard_map/ppermute | solution.py:28
  42.9 4.0 %collective-permute-start.9 = (f32[5,1,1,130]{3,2,1,0:T(1,128)S(1)}, f32[5,1,1,130]{3,2,1,0:T(1,128)S(1)}, u32[]{:S(2)}, u32[]{:S(2)}) collective-permute-start(f32[5,1,1,130]{3,2,1,0:T(1,128)S(1)} %get-tuple-element.12), channel_id=1, source_target_pairs={{0,1},{1,2},{2,3},{3,4},{4,5},{5,6},{6,7},{7,0},{8,9},{9,10},{10,1... | collective-permute-start | bytes 7808 | tf_op jit(solution)/shard_map/ppermute | solution.py:27
  47.8 11.2 %collective-permute-start.11 = (f32[5,1,64,128]{3,2,1,0:T(8,128)S(1)}, f32[5,1,64,128]{3,2,1,0:T(8,128)S(1)}, u32[]{:S(2)}, u32[]{:S(2)}) collective-permute-start(f32[5,1,64,128]{3,2,1,0:T(8,128)S(1)} %fusion.25), channel_id=1, source_target_pairs={{0,3},{1,4},{2,5},{3,6},{4,7},{5,0},{6,1},{7,2},{8,11},{9,12},{10,... | collective-permute-start | bytes 491528 | tf_op jit(solution)/shard_map/ppermute | solution.py:17
  47.9 11.2 %collective-permute-start.12 = (f32[5,1,64,128]{3,2,1,0:T(8,128)S(1)}, f32[5,1,64,128]{3,2,1,0:T(8,128)S(1)}, u32[]{:S(2)}, u32[]{:S(2)}) collective-permute-start(f32[5,1,64,128]{3,2,1,0:T(8,128)S(1)} %fusion.25), channel_id=1, source_target_pairs={{0,2},{1,3},{2,4},{3,5},{4,6},{5,7},{6,0},{7,1},{8,10},{9,11},{10,... | collective-permute-start | bytes 491528 | tf_op jit(solution)/shard_map/ppermute | solution.py:17
  48.1 11.0 %collective-permute-start.13 = (f32[5,1,64,128]{3,2,1,0:T(8,128)S(1)}, f32[5,1,64,128]{3,2,1,0:T(8,128)S(1)}, u32[]{:S(2)}, u32[]{:S(2)}) collective-permute-start(f32[5,1,64,128]{3,2,1,0:T(8,128)S(1)} %fusion.25), channel_id=1, source_target_pairs={{0,1},{1,2},{2,3},{3,4},{4,5},{5,6},{6,7},{7,0},{8,9},{9,10},{10,1... | collective-permute-start | bytes 491528 | tf_op jit(solution)/shard_map/ppermute | solution.py:17
  60.6 6.3 %collective-permute-start.14 = (f32[5,1,64,1]{3,2,1,0:T(8,128)S(1)}, f32[5,1,64,1]{3,2,1,0:T(8,128)S(1)}, u32[]{:S(2)}, u32[]{:S(2)}) collective-permute-start(f32[5,1,64,1]{3,2,1,0:T(8,128)S(1)} %get-tuple-element.18), channel_id=1, source_target_pairs={{0,8},{8,16},{16,24},{1,9},{9,17},{17,25},{2,10},{10,18},{18,26},{... | collective-permute-start | bytes 3848 | tf_op jit(solution)/shard_map/ppermute | solution.py:27
  64.0 7.2 %collective-permute-start.15 = (f32[5,1,64,1]{3,2,1,0:T(8,128)S(1)}, f32[5,1,64,1]{3,2,1,0:T(8,128)S(1)}, u32[]{:S(2)}, u32[]{:S(2)}) collective-permute-start(f32[5,1,64,1]{3,2,1,0:T(8,128)S(1)} %get-tuple-element.17), channel_id=1, source_target_pairs={{8,0},{16,8},{24,16},{9,1},{17,9},{25,17},{10,2},{18,10},{26,18},{... | collective-permute-start | bytes 3848 | tf_op jit(solution)/shard_map/ppermute | solution.py:28
  71.4 4.0 %collective-permute-start.16 = (f32[5,1,1,130]{3,2,1,0:T(1,128)S(1)}, f32[5,1,1,130]{3,2,1,0:T(1,128)S(1)}, u32[]{:S(2)}, u32[]{:S(2)}) collective-permute-start(f32[5,1,1,130]{3,2,1,0:T(1,128)S(1)} %get-tuple-element.8), channel_id=1, source_target_pairs={{0,1},{1,2},{2,3},{3,4},{4,5},{5,6},{6,7},{7,0},{8,9},{9,10},{10,1... | collective-permute-start | bytes 7808 | tf_op jit(solution)/shard_map/ppermute | solution.py:27
  71.4 4.0 %collective-permute-start.17 = (f32[5,1,1,130]{3,2,1,0:T(1,128)S(1)}, f32[5,1,1,130]{3,2,1,0:T(1,128)S(1)}, u32[]{:S(2)}, u32[]{:S(2)}) collective-permute-start(f32[5,1,1,130]{3,2,1,0:T(1,128)S(1)} %get-tuple-element.7), channel_id=1, source_target_pairs={{1,0},{2,1},{3,2},{4,3},{5,4},{6,5},{7,6},{0,7},{9,8},{10,9},{11,1... | collective-permute-start | bytes 7808 | tf_op jit(solution)/shard_map/ppermute | solution.py:28
  76.3 11.5 %collective-permute-start.18 = (f32[5,1,64,128]{3,2,1,0:T(8,128)S(1)}, f32[5,1,64,128]{3,2,1,0:T(8,128)S(1)}, u32[]{:S(2)}, u32[]{:S(2)}) collective-permute-start(f32[5,1,64,128]{3,2,1,0:T(8,128)S(1)} %fusion.10), channel_id=1, source_target_pairs={{0,3},{1,4},{2,5},{3,6},{4,7},{5,0},{6,1},{7,2},{8,11},{9,12},{10,... | collective-permute-start | bytes 491528 | tf_op jit(solution)/shard_map/ppermute | solution.py:17
  78.3 9.5 %collective-permute-start.19 = (f32[5,1,64,128]{3,2,1,0:T(8,128)S(1)}, f32[5,1,64,128]{3,2,1,0:T(8,128)S(1)}, u32[]{:S(2)}, u32[]{:S(2)}) collective-permute-start(f32[5,1,64,128]{3,2,1,0:T(8,128)S(1)} %fusion.10), channel_id=1, source_target_pairs={{0,2},{1,3},{2,4},{3,5},{4,6},{5,7},{6,0},{7,1},{8,10},{9,11},{10,... | collective-permute-start | bytes 491528 | tf_op jit(solution)/shard_map/ppermute | solution.py:17
  78.3 9.5 %collective-permute-start.20 = (f32[5,1,64,128]{3,2,1,0:T(8,128)S(1)}, f32[5,1,64,128]{3,2,1,0:T(8,128)S(1)}, u32[]{:S(2)}, u32[]{:S(2)}) collective-permute-start(f32[5,1,64,128]{3,2,1,0:T(8,128)S(1)} %fusion.10), channel_id=1, source_target_pairs={{0,1},{1,2},{2,3},{3,4},{4,5},{5,6},{6,7},{7,0},{8,9},{9,10},{10,1... | collective-permute-start | bytes 491528 | tf_op jit(solution)/shard_map/ppermute | solution.py:17
where the time goes:
time: 90.1 us; the launch traced here: 89.8 us
  waiting for transfers between devices  50.8 us (56%)
  starting transfers between devices  28.8 us (32%)
  other arithmetic  5.04 us (6%)
  local copies, waits for them, and re-layouts  4.55 us (5%)
    ppermute x9, waiting for transfers between devices, passed_along(): return lax.ppermute(value, axis, pairs)  27.4 us
    ppermute x6, waiting for transfers between devices, padded_2(): after = lax.ppermute(initial, axis, down)  13.8 us
    ppermute x6, starting transfers between devices, padded_2(): before = lax.ppermute(last, axis, up)  12.5 us
    ppermute x6, waiting for transfers between devices, padded_2(): before = lax.ppermute(last, axis, up)  9.57 us
    ppermute x6, starting transfers between devices, padded_2(): after = lax.ppermute(initial, axis, down)  9.2 us
    ppermute x9, starting transfers between devices, passed_along(): return lax.ppermute(value, axis, pairs)  7.13 us
    concatenate x3, local copies, waits for them, and re-layouts, rotate_pieces(): window = jnp.concatenate([front, extended], axis=2)  2.5 us
    select_n x24, other arithmetic, rotate_pieces(): jnp.where(chosen[None, None, None, :], window[:, :, :length], window[:, :...  2.07 us
  transfers between devices with their start and end apart: 21, of which 15 were waited for; matrix products, arithmetic and copies ran while one was open for 0% of the time, Pallas kernels for 0%

commit v1 on v0

--- a/solution.py
+++ b/solution.py
@@ -1,14 +1,283 @@
+import functools
+
 import jax
 import jax.numpy as jnp
 from jax import lax
+from jax.experimental import pallas as pl
+from jax.experimental.pallas import tpu as pltpu
 from jax.sharding import PartitionSpec as P
 
 STEPS = 3
 SMAX = 192
-
+FIELDS = 5
+LANES = 128
+SUB = 8
+HALF = 64
 
 courant = 0.2
 viscous = 0.1
+
+
+def halves(a, b, low):
+    first = jnp.where(low, a, pltpu.roll(b, HALF, b.ndim - 1))
+    second = jnp.where(low, pltpu.roll(a, HALF, a.ndim - 1), b)
+    return first, second
+
+
+def step_update(f, inverse):
+    inner = [pltpu.roll(u, 1, 0) for u in f]
+    outer = [pltpu.roll(u, u.shape[0] - 1, 0) for u in f]
+    behind = [pltpu.roll(u, 1, 1) for u in f]
+    ahead = [pltpu.roll(u, u.shape[1] - 1, 1) for u in f]
+    log_rho, vr, vp, _, temper = f
+    r_pos = courant * jnp.maximum(vr, 0.0)
+    r_neg = courant * jnp.minimum(vr, 0.0)
+    cg = courant * inverse
+    p_pos = cg * jnp.maximum(vp, 0.0)
+    p_neg = cg * jnp.minimum(vp, 0.0)
+    vg2 = viscous * inverse * inverse
+
+    def moved(i):
+        u = f[i]
+        d_in, d_out = u - inner[i], outer[i] - u
+        d_back, d_fwd = u - behind[i], ahead[i] - u
+        base = u - (r_pos * d_in + r_neg * d_out + p_pos * d_back + p_neg * d_fwd)
+        if i == 0:
+            return base
+        polar = (u + u) - 2.0 * u
+        return base + (viscous * ((d_out - d_in) + polar) + vg2 * (d_fwd - d_back))
+
+    def dr(i):
+        return (outer[i] - inner[i]) * 0.5
+
+    def dp(i):
+        return (ahead[i] - behind[i]) * 0.5
+
+    diverge = dr(1) + inverse * dp(2)
+    new_log = moved(0) - courant * diverge
+    new_vr = moved(1) - courant * (temper * dr(0) + dr(4)) + (0.5 * cg) * vp * vp
+    new_vp = moved(2) - cg * (temper * dp(0) + dp(4)) - (0.5 * cg) * vr * vp
+    new_vz = moved(3)
+    new_t = moved(4) - (courant * 0.4) * temper * diverge
+    return [new_log, new_vr, new_vp, new_vz, new_t]
+
+
+def rotate(u, index, lag):
+    tiles = u.shape[1] // LANES
+    g = [
+        jnp.take_along_axis(u[:, q * LANES : (q + 1) * LANES], index, axis=1)
+        for q in range(tiles)
+    ]
+    out = []
+    for q in range(tiles):
+        value = g[(q - (SMAX // LANES + 1)) % tiles]
+        for back in range(SMAX // LANES, -1, -1):
+            value = jnp.where(lag == back, g[(q - back) % tiles], value)
+        out.append(value)
+    return jnp.concatenate(out, axis=1)
+
+
+def kernel(
+    n, nr, f_ref, s_ref, o_ref, z, send, recv, edge, send2, recv2,
+    ssem, rsem, esend, erecv, ssem2, rsem2,
+):
+    r = lax.axis_index("rad")
+    t = lax.axis_index("azi")
+    tiles = f_ref.shape[3] // SUB
+    peers = [lax.rem(t + d, n) for d in range(1, n)]
+    top_edge = (t == 0) & (r > 0)
+    bottom_edge = (t == n - 1) & (r < nr - 1)
+
+    barrier = pltpu.get_barrier_semaphore()
+    for peer in peers:
+        pl.semaphore_signal(barrier, inc=1, device_id={"azi": peer})
+
+    @pl.when(top_edge)
+    def _():
+        for b in range(n):
+            pl.semaphore_signal(barrier, inc=1, device_id={"rad": r - 1, "azi": b})
+
+    @pl.when(bottom_edge)
+    def _():
+        for b in range(n):
+            pl.semaphore_signal(barrier, inc=1, device_id={"rad": r + 1, "azi": b})
+
+    sub = lax.broadcasted_iota(jnp.int32, (SUB, LANES), 0)
+    lane = lax.broadcasted_iota(jnp.int32, (SUB, LANES), 1)
+    low = lane < HALF
+
+    shifts = s_ref[...].astype(jnp.float32)
+    rest = jnp.zeros((HALF - STEPS, LANES), jnp.float32)
+    stacks = [
+        f_ref[0:2, 0].reshape(LANES, LANES),
+        f_ref[2:4, 0].reshape(LANES, LANES),
+        jnp.concatenate([f_ref[4, 0], shifts, rest], axis=0),
+    ]
+    for p, stack in enumerate(stacks):
+        z[:, p] = stack.T.reshape(tiles, SUB, LANES)
+
+    for k in range(n):
+        a, b = 2 * k, 2 * k + 1
+        for p in range(2):
+            send[k, 2 * p] = z[a, p]
+            send[k, 2 * p + 1] = z[b, p]
+        send[k, 4] = jnp.where(low, z[a, 2], pltpu.roll(z[b, 2], HALF, 1))
+        above, below = max(a - 1, 0), min(b + 1, tiles - 1)
+        for p in range(3):
+            send[k, 5 + p] = jnp.where(sub >= SUB - STEPS, z[above, p], z[below, p])
+
+    needed = n - 1 + (r > 0).astype(jnp.int32) + (r < nr - 1).astype(jnp.int32)
+    pl.semaphore_wait(barrier, needed)
+
+    def edge_copy(which, row, slot, device):
+        return pltpu.make_async_remote_copy(
+            src_ref=z.at[row], dst_ref=edge.at[slot], send_sem=esend.at[which],
+            recv_sem=erecv.at[slot], device_id=device,
+        )
+
+    to_inner = edge_copy(0, 0, t, {"rad": r - 1, "azi": n - 1})
+    to_outer = edge_copy(1, tiles - 1, t, {"rad": r + 1, "azi": 0})
+
+    @pl.when(r > 0)
+    def _():
+        to_inner.start()
+
+    @pl.when(r < nr - 1)
+    def _():
+        to_outer.start()
+
+    copies = []
+    for d, peer in enumerate(peers):
+        copy = pltpu.make_async_remote_copy(
+            src_ref=send.at[peer], dst_ref=recv.at[t], send_sem=ssem.at[d],
+            recv_sem=rsem.at[d], device_id={"azi": peer},
+        )
+        copy.start()
+        copies.append(copy)
+    recv[t] = send[t]
+
+    rows = 3 * SUB
+    width = n * HALF
+    row = lax.broadcasted_iota(jnp.int32, (rows, width), 0)
+    row = jnp.where(row < 2 * SUB + SUB // 2, row, row - rows)
+    row = row + (r * f_ref.shape[3] + t * (2 * SUB))
+    total = nr * f_ref.shape[3]
+    inside = (row >= 0) & (row < total)
+    radius = 1.0 + (row.astype(jnp.float32) + 0.5) / jnp.float32(total)
+    inverse = 1.0 / radius
+
+    for copy in copies:
+        copy.wait_recv()
+
+    @pl.when(top_edge | bottom_edge)
+    def _():
+        first = jnp.where(t == 0, SUB - STEPS, 0)
+        last = jnp.where(t == 0, SUB, STEPS)
+        take = (sub >= first) & (sub < last)
+        for b in range(n):
+            edge_copy(0, 0, b, {"rad": lax.rem(r + 1, nr), "azi": 0}).wait_recv()
+            for p in range(3):
+                recv[b, 5 + p] = jnp.where(take, edge[b, p], recv[b, 5 + p])
+
+    fields = [[] for _ in range(FIELDS)]
+    for q in range(n // 2):
+        got = [halves(recv[2 * q, i], recv[2 * q + 1, i], low) for i in range(8)]
+        for p in range(2):
+            for h in range(2):
+                fields[2 * p + h].append(
+                    jnp.concatenate([got[2 * p][h], got[2 * p + 1][h], got[5 + p][h]], axis=0)
+                )
+        fields[4].append(jnp.concatenate([got[4][0], got[4][1], got[7][0]], axis=0))
+    fields = [jnp.where(inside, jnp.concatenate(u, axis=1), 0.0) for u in fields]
+
+    carried = jnp.concatenate([z[2 * t, 2], z[2 * t + 1, 2], recv[0, 7]], axis=0)
+    lanes = lax.broadcasted_iota(jnp.int32, (rows, LANES), 1)
+    for step in range(STEPS):
+        shift = carried[:, HALF + step : HALF + step + 1].astype(jnp.int32)
+        shift = jnp.broadcast_to(shift, (rows, LANES))
+        whole = jnp.where(shift >= LANES, 1, 0)
+        part = shift - whole * LANES
+        index = jnp.bitwise_and(lanes - part, LANES - 1)
+        lag = whole + jnp.where(lanes < part, 1, 0)
+        fields = [jnp.where(inside, u, 0.0) for u in step_update(fields, inverse)]
+        fields = [rotate(u, index, lag) for u in fields]
+
+    for q in range(n // 2):
+        f = [u[:, q * LANES : (q + 1) * LANES] for u in fields]
+        for p in range(2):
+            for i in range(2):
+                rs = slice(i * SUB, (i + 1) * SUB)
+                even, odd = halves(f[2 * p][rs], f[2 * p + 1][rs], low)
+                send2[2 * q, 2 * p + i] = even
+                send2[2 * q + 1, 2 * p + i] = odd
+        even, odd = halves(f[4][:SUB], f[4][SUB : 2 * SUB], low)
+        send2[2 * q, 4] = even
+        send2[2 * q + 1, 4] = odd
+
+    backs = []
+    for d, peer in enumerate(peers):
+        copy = pltpu.make_async_remote_copy(
+            src_ref=send2.at[peer], dst_ref=recv2.at[t], send_sem=ssem2.at[d],
+            recv_sem=rsem2.at[d], device_id={"azi": peer},
+        )
+        copy.start()
+        backs.append(copy)
+    recv2[t] = send2[t]
+
+    for copy in copies:
+        copy.wait_send()
+
+    @pl.when(r > 0)
+    def _():
+        to_inner.wait_send()
+
+    @pl.when(r < nr - 1)
+    def _():
+        to_outer.wait_send()
+
+    for copy in backs:
+        copy.wait_recv()
+
+    for p in range(2):
+        block = recv2[:, 2 * p : 2 * p + 2].reshape(LANES, LANES)
+        o_ref[2 * p : 2 * p + 2, 0] = block.T.reshape(2, HALF, LANES)
+    parts = []
+    for b in range(n):
+        tile = recv2[b, 4]
+        parts += [tile, pltpu.roll(tile, HALF, 1)]
+    o_ref[4, 0] = jnp.concatenate(parts, axis=0).T[:HALF]
+
+    for copy in backs:
+        copy.wait_send()
+
+
+def by_cycles(n, nr, fields, shifts):
+    tiles = fields.shape[3] // SUB
+    tile = (SUB, LANES)
+    dma = pltpu.SemaphoreType.DMA
+    return pl.pallas_call(
+        functools.partial(kernel, n, nr),
+        out_shape=jax.ShapeDtypeStruct(fields.shape, fields.dtype),
+        in_specs=[pl.BlockSpec(memory_space=pltpu.VMEM)] * 2,
+        out_specs=pl.BlockSpec(memory_space=pltpu.VMEM),
+        scratch_shapes=[
+            pltpu.VMEM((tiles, 3) + tile, jnp.float32),
+            pltpu.VMEM((n, 8) + tile, jnp.float32),
+            pltpu.VMEM((n, 8) + tile, jnp.float32),
+            pltpu.VMEM((n, 3) + tile, jnp.float32),
+            pltpu.VMEM((n, 5) + tile, jnp.float32),
+            pltpu.VMEM((n, 5) + tile, jnp.float32),
+            dma((n - 1,)),
+            dma((n - 1,)),
+            dma((2,)),
+            dma((n,)),
+            dma((n - 1,)),
+            dma((n - 1,)),
+        ],
+        compiler_params=pltpu.CompilerParams(
+            collective_id=0, has_side_effects=True, vmem_limit_bytes=16 * 1024 * 1024
+        ),
+    )(fields, shifts)
 
 
 def passed_along(value, axis, steps):
@@ -103,7 +372,7 @@
     return window
 
 
-def local(fields, shifts):
+def by_blocks(fields, shifts):
     rows = fields.shape[3]
     total_rows = rows * lax.axis_size("rad")
     row_index = lax.axis_index("rad") * rows + jnp.arange(rows, dtype=jnp.int32)
@@ -117,6 +386,15 @@
     return fields
 
 
+def local(fields, shifts):
+    n, nr = lax.axis_size("azi"), lax.axis_size("rad")
+    count, planes, width, rows = fields.shape
+    fits = (count, planes, width, rows) == (FIELDS, 1, HALF, LANES)
+    if fits and rows == n * 2 * SUB and n * width > SMAX + LANES:
+        return by_cycles(n, nr, fields, shifts)
+    return by_blocks(fields, shifts)
+
+
 def solution(mesh):
     placed = (P(None, None, "azi", "rad"), P(None, "rad"))
     return jax.shard_map(

time: 90.1 us -> 16.7 us (0.19)
  waiting for transfers between devices: 50.8 us -> 0 us
  starting transfers between devices: 28.8 us -> 0 us
  Pallas kernels: 0 us -> 14.2 us
  other arithmetic: 5.04 us -> 0 us
  local copies, waits for them, and re-layouts: 4.55 us -> 2.27 us
    ppermute x21 -> x0, waiting for transfers between devices: 50.8 us -> none  [the longest x9 27.4 us: passed_along(): return lax.ppermute(value, axis, pairs)]
    ppermute x21 -> x0, starting transfers between devices: 28.8 us -> none  [the longest x6 12.5 us: padded_2(): before = lax.ppermute(last, axis, up)]
    pallas_call x0 -> x1, Pallas kernels: none -> 14.2 us  [by_cycles(): pl.pallas_call(functools.partial(kernel, n, nr), out_shape=jax.ShapeDtype...]
    concatenate x3 -> x0, local copies, waits for them, and re-layouts: 2.5 us -> none  [rotate_pieces(): window = jnp.concatenate([front, extended], axis=2)]
    select_n x24 -> x0, other arithmetic: 2.07 us -> none  [rotate_pieces(): jnp.where(chosen[None, None, None, :], window[:, :, :length], window[:, :...]
    unnamed x4 -> x5, local copies, waits for them, and re-layouts: 0.68 us -> 2.27 us
    mul x10 -> x0, other arithmetic: 1.44 us -> none  [the longest x3 0.89 us: update(): courant * (jnp.maximum(radial_vel, 0.0) * (centre - inner) + jnp.minimum(...]
    slice x3 -> x0, local copies, waits for them, and re-layouts: 1.36 us -> none  [padded_2(): initial = lax.slice_in_dim(value, 0, width, axis=dim)]
  transfers between devices with their start and end apart: 21 -> 0, of which waited for: 15 -> 0; matrix products, arithmetic and copies ran while one was open for 0% -> 0% of each run, Pallas kernels for 0% -> 0%
where the time goes in v1:
time: 16.7 us; the launch traced here: 16.5 us
  Pallas kernels  14.2 us (85%)
  local copies, waits for them, and re-layouts  2.27 us (14%)
    pallas_call x1, Pallas kernels, by_cycles(): pl.pallas_call(functools.partial(kernel, n, nr), out_shape=jax.ShapeDtype...  14.2 us
    unnamed x5, local copies, waits for them, and re-layouts  2.27 us

profile of v1, /device:TPU:0, one launch (start us, length us, event | category | flops | bytes accessed | tf_op | source)
XLA Modules:
  0.0 16.5 jit_solution(16913137776115955061)
XLA Ops:
  0.0 0.0 copy-start
  0.0 0.9 %copy-done = f32[5,1,64,128]{3,2,1,0:T(8,128)S(1)} copy-done((f32[5,1,64,128]{3,2,1,0:T(8,128)S(1)}, f32[5,1,64,128]{3,2,1,0:T(8,128)}, u32[]{:S(2)}) %copy-start) | copy-done | bytes 163864
  0.9 0.0 copy-start.1
  0.9 0.7 %copy-done.1 = s32[3,128]{1,0:T(4,128)S(1)} copy-done((s32[3,128]{1,0:T(4,128)S(1)}, s32[3,128]{1,0:T(4,128)}, u32[]{:S(2)}) %copy-start.1) | copy-done | bytes 1560
  1.6 14.2 %shard_map.28 = f32[5,1,64,128]{3,2,1,0:T(8,128)S(1)} custom-call(f32[5,1,64,128]{3,2,1,0:T(8,128)S(1)} %copy-done, s32[3,128]{1,0:T(4,128)S(1)} %copy-done.1), custom_call_target="tpu_custom_call" | custom-call | tf_op jit(solution)/shard_map/pallas_call | solution.py:258
  15.9 0.7 %copy.4 = f32[5,1,64,128]{3,2,1,0:T(8,128)} copy(f32[5,1,64,128]{3,2,1,0:T(8,128)S(1)} %shard_map.28) | data formatting | bytes 327680
Async XLA Ops:
  0.0 0.9 %copy-start = (f32[5,1,64,128]{3,2,1,0:T(8,128)S(1)}, f32[5,1,64,128]{3,2,1,0:T(8,128)}, u32[]{:S(2)}) copy-start(f32[5,1,64,128]{3,2,1,0:T(8,128)} %f_ref.1) | copy-start | bytes 491524
  0.9 0.7 %copy-start.1 = (s32[3,128]{1,0:T(4,128)S(1)}, s32[3,128]{1,0:T(4,128)}, u32[]{:S(2)}) copy-start(s32[3,128]{1,0:T(4,128)} %s_ref.1) | copy-start | bytes 4612

commit v2 on v1

--- a/solution.py
+++ b/solution.py
@@ -78,9 +78,13 @@
 
 
 def kernel(
-    n, nr, f_ref, s_ref, o_ref, z, send, recv, edge, send2, recv2,
-    ssem, rsem, esend, erecv, ssem2, rsem2,
+    n, nr, f_hbm, s_hbm, o_ref, f_ref, s_ref, z, send, recv, edge, send2, recv2,
+    ssem, rsem, esend, erecv, ssem2, rsem2, isem,
 ):
+    f_in = pltpu.make_async_copy(f_hbm, f_ref, isem.at[0])
+    s_in = pltpu.make_async_copy(s_hbm, s_ref, isem.at[1])
+    f_in.start()
+    s_in.start()
     r = lax.axis_index("rad")
     t = lax.axis_index("azi")
     tiles = f_ref.shape[3] // SUB
@@ -106,6 +110,8 @@
     lane = lax.broadcasted_iota(jnp.int32, (SUB, LANES), 1)
     low = lane < HALF
 
+    s_in.wait()
+    f_in.wait()
     shifts = s_ref[...].astype(jnp.float32)
     rest = jnp.zeros((HALF - STEPS, LANES), jnp.float32)
     stacks = [
@@ -258,9 +264,11 @@
     return pl.pallas_call(
         functools.partial(kernel, n, nr),
         out_shape=jax.ShapeDtypeStruct(fields.shape, fields.dtype),
-        in_specs=[pl.BlockSpec(memory_space=pltpu.VMEM)] * 2,
+        in_specs=[pl.BlockSpec(memory_space=pltpu.HBM)] * 2,
         out_specs=pl.BlockSpec(memory_space=pltpu.VMEM),
         scratch_shapes=[
+            pltpu.VMEM(fields.shape, fields.dtype),
+            pltpu.VMEM(shifts.shape, shifts.dtype),
             pltpu.VMEM((tiles, 3) + tile, jnp.float32),
             pltpu.VMEM((n, 8) + tile, jnp.float32),
             pltpu.VMEM((n, 8) + tile, jnp.float32),
@@ -273,6 +281,7 @@
             dma((n,)),
             dma((n - 1,)),
             dma((n - 1,)),
+            dma((2,)),
         ],
         compiler_params=pltpu.CompilerParams(
             collective_id=0, has_side_effects=True, vmem_limit_bytes=16 * 1024 * 1024

time: 16.7 us -> 16.9 us (1.012)
  Pallas kernels: 14.2 us -> 14.5 us
    pallas_call x1, Pallas kernels: 14.2 us -> 14.5 us  [by_cycles(): pl.pallas_call(functools.partial(kernel, n, nr), out_shape=jax.ShapeDtype...]
where the time goes in v2:
time: 16.9 us; the launch traced here: 16.8 us
  Pallas kernels  14.5 us (86%)
  local copies, waits for them, and re-layouts  2.27 us (13%)
    pallas_call x1, Pallas kernels, by_cycles(): pl.pallas_call(functools.partial(kernel, n, nr), out_shape=jax.ShapeDtype...  14.5 us
    unnamed x5, local copies, waits for them, and re-layouts  2.27 us

profile of v2, /device:TPU:0, one launch (start us, length us, event | category | flops | bytes accessed | tf_op | source)
XLA Modules:
  0.0 16.8 jit_solution(13897836637992462591)
XLA Ops:
  0.0 0.0 copy-start
  0.0 0.9 %copy-done = f32[5,1,64,128]{3,2,1,0:T(8,128)S(1)} copy-done((f32[5,1,64,128]{3,2,1,0:T(8,128)S(1)}, f32[5,1,64,128]{3,2,1,0:T(8,128)}, u32[]{:S(2)}) %copy-start) | copy-done | bytes 163864
  0.9 0.0 copy-start.1
  0.9 0.7 %copy-done.1 = s32[3,128]{1,0:T(4,128)S(1)} copy-done((s32[3,128]{1,0:T(4,128)S(1)}, s32[3,128]{1,0:T(4,128)}, u32[]{:S(2)}) %copy-start.1) | copy-done | bytes 1560
  1.6 14.5 %shard_map.28 = f32[5,1,64,128]{3,2,1,0:T(8,128)S(1)} custom-call(f32[5,1,64,128]{3,2,1,0:T(8,128)S(1)} %copy-done, s32[3,128]{1,0:T(4,128)S(1)} %copy-done.1), custom_call_target="tpu_custom_call" | custom-call | tf_op jit(solution)/shard_map/pallas_call | solution.py:264
  16.1 0.7 %copy.4 = f32[5,1,64,128]{3,2,1,0:T(8,128)} copy(f32[5,1,64,128]{3,2,1,0:T(8,128)S(1)} %shard_map.28) | data formatting | bytes 327680
Async XLA Ops:
  0.0 0.9 %copy-start = (f32[5,1,64,128]{3,2,1,0:T(8,128)S(1)}, f32[5,1,64,128]{3,2,1,0:T(8,128)}, u32[]{:S(2)}) copy-start(f32[5,1,64,128]{3,2,1,0:T(8,128)} %f_hbm.1) | copy-start | bytes 491524
  0.9 0.7 %copy-start.1 = (s32[3,128]{1,0:T(4,128)S(1)}, s32[3,128]{1,0:T(4,128)}, u32[]{:S(2)}) copy-start(s32[3,128]{1,0:T(4,128)} %s_hbm.1) | copy-start | bytes 4612

commit v3 on v2

--- a/solution.py
+++ b/solution.py
@@ -78,7 +78,7 @@
 
 
 def kernel(
-    n, nr, f_hbm, s_hbm, o_ref, f_ref, s_ref, z, send, recv, edge, send2, recv2,
+    n, nr, f_hbm, s_hbm, recv2, f_ref, s_ref, z, send, recv, edge, send2,
     ssem, rsem, esend, erecv, ssem2, rsem2, isem,
 ):
     f_in = pltpu.make_async_copy(f_hbm, f_ref, isem.at[0])
@@ -244,26 +244,38 @@
     for copy in backs:
         copy.wait_recv()
 
-    for p in range(2):
-        block = recv2[:, 2 * p : 2 * p + 2].reshape(LANES, LANES)
-        o_ref[2 * p : 2 * p + 2, 0] = block.T.reshape(2, HALF, LANES)
-    parts = []
-    for b in range(n):
-        tile = recv2[b, 4]
-        parts += [tile, pltpu.roll(tile, HALF, 1)]
-    o_ref[4, 0] = jnp.concatenate(parts, axis=0).T[:HALF]
-
     for copy in backs:
         copy.wait_send()
+
+
+def to_cells(got, o_hbm, out, sem):
+    n = got.shape[0]
+    writes = []
+    for p in range(3):
+        fs = slice(2 * p, min(2 * p + 2, FIELDS))
+        if p < 2:
+            block = got[:, 2 * p : 2 * p + 2].reshape(LANES, LANES)
+            out[fs, 0] = block.T.reshape(2, HALF, LANES)
+        else:
+            parts = []
+            for b in range(n):
+                tile = got[b, 4]
+                parts += [tile, pltpu.roll(tile, HALF, 1)]
+            out[4, 0] = jnp.concatenate(parts, axis=0).T[:HALF]
+        write = pltpu.make_async_copy(out.at[fs], o_hbm.at[fs], sem.at[p])
+        write.start()
+        writes.append(write)
+    for write in writes:
+        write.wait()
 
 
 def by_cycles(n, nr, fields, shifts):
     tiles = fields.shape[3] // SUB
     tile = (SUB, LANES)
     dma = pltpu.SemaphoreType.DMA
-    return pl.pallas_call(
+    got = pl.pallas_call(
         functools.partial(kernel, n, nr),
-        out_shape=jax.ShapeDtypeStruct(fields.shape, fields.dtype),
+        out_shape=pltpu.VMEM((n, 5) + tile, jnp.float32),
         in_specs=[pl.BlockSpec(memory_space=pltpu.HBM)] * 2,
         out_specs=pl.BlockSpec(memory_space=pltpu.VMEM),
         scratch_shapes=[
@@ -273,7 +285,6 @@
             pltpu.VMEM((n, 8) + tile, jnp.float32),
             pltpu.VMEM((n, 8) + tile, jnp.float32),
             pltpu.VMEM((n, 3) + tile, jnp.float32),
-            pltpu.VMEM((n, 5) + tile, jnp.float32),
             pltpu.VMEM((n, 5) + tile, jnp.float32),
             dma((n - 1,)),
             dma((n - 1,)),
@@ -286,7 +297,18 @@
         compiler_params=pltpu.CompilerParams(
             collective_id=0, has_side_effects=True, vmem_limit_bytes=16 * 1024 * 1024
         ),
-    )(fields, shifts)
+    )(
+        pltpu.with_memory_space_constraint(fields, pltpu.HBM),
+        pltpu.with_memory_space_constraint(shifts, pltpu.HBM),
+    )
+    return pl.pallas_call(
+        to_cells,
+        out_shape=jax.ShapeDtypeStruct(fields.shape, fields.dtype),
+        in_specs=[pl.BlockSpec(memory_space=pltpu.VMEM)],
+        out_specs=pl.BlockSpec(memory_space=pltpu.HBM),
+        scratch_shapes=[pltpu.VMEM(fields.shape, fields.dtype), dma((3,))],
+        compiler_params=pltpu.CompilerParams(vmem_limit_bytes=16 * 1024 * 1024),
+    )(got)
 
 
 def passed_along(value, axis, steps):

time: 16.9 us -> 15.1 us (0.89)
  local copies, waits for them, and re-layouts: 2.27 us -> 0 us
  Pallas kernels: 14.5 us -> 14.9 us
    unnamed x5 -> x0, local copies, waits for them, and re-layouts: 2.27 us -> none
    pallas_call x1 -> x2, Pallas kernels: 14.5 us -> 14.9 us  [the longest x1 14.1 us: by_cycles(): pl.pallas_call(functools.partial(kernel, n, nr), out_shape=pltpu.VMEM((n,...]
where the time goes in v3:
time: 15.1 us; the launch traced here: 14.9 us
  Pallas kernels  14.9 us (99%)
    pallas_call x1, Pallas kernels, by_cycles(): pl.pallas_call(functools.partial(kernel, n, nr), out_shape=pltpu.VMEM((n,...  14.1 us
    pallas_call x1, Pallas kernels, by_cycles(): pl.pallas_call(to_cells, out_shape=jax.ShapeDtypeStruct(fields.shape, fie...  0.8 us

profile of v3, /device:TPU:0, one launch (start us, length us, event | category | flops | bytes accessed | tf_op | source)
XLA Modules:
  0.0 14.9 jit_solution(16795808176897219972)
XLA Ops:
  0.0 14.1 %shard_map.28.got = f32[8,5,8,128]{3,2,1,0:T(8,128)S(1)} custom-call(f32[5,1,64,128]{3,2,1,0:T(8,128)} %f_hbm.1, s32[3,128]{1,0:T(4,128)} %s_hbm.1), custom_call_target="tpu_custom_call" | custom-call | tf_op jit(solution)/shard_map/pallas_call | solution.py:276
  14.1 0.8 %shard_map.29 = f32[5,1,64,128]{3,2,1,0:T(8,128)} custom-call(f32[8,5,8,128]{3,2,1,0:T(8,128)S(1)} %shard_map.28.got), custom_call_target="tpu_custom_call" | custom-call | tf_op jit(solution)/shard_map/pallas_call | solution.py:304

commit v4 on v3

--- a/solution.py
+++ b/solution.py
@@ -13,6 +13,9 @@
 LANES = 128
 SUB = 8
 HALF = 64
+PAIRS = (slice(0, 2), slice(2, 4), slice(4, 5))
+THERE = (slice(0, 3), slice(3, 6), slice(6, 8))
+BACK = (slice(0, 2), slice(2, 4), slice(4, 5))
 
 courant = 0.2
 viscous = 0.1
@@ -24,12 +27,14 @@
     return first, second
 
 
-def step_update(f, inverse):
-    inner = [pltpu.roll(u, 1, 0) for u in f]
-    outer = [pltpu.roll(u, u.shape[0] - 1, 0) for u in f]
+def updates(f, inverse, rows):
+    inner = [pltpu.roll(u, 1, 0)[:rows] for u in f]
+    outer = [pltpu.roll(u, u.shape[0] - 1, 0)[:rows] for u in f]
+    f = [u[:rows] for u in f]
+    inverse = inverse[:rows]
     behind = [pltpu.roll(u, 1, 1) for u in f]
     ahead = [pltpu.roll(u, u.shape[1] - 1, 1) for u in f]
-    log_rho, vr, vp, _, temper = f
+    _, vr, vp, _, temper = f
     r_pos = courant * jnp.maximum(vr, 0.0)
     r_neg = courant * jnp.minimum(vr, 0.0)
     cg = courant * inverse
@@ -54,12 +59,13 @@
         return (ahead[i] - behind[i]) * 0.5
 
     diverge = dr(1) + inverse * dp(2)
-    new_log = moved(0) - courant * diverge
-    new_vr = moved(1) - courant * (temper * dr(0) + dr(4)) + (0.5 * cg) * vp * vp
-    new_vp = moved(2) - cg * (temper * dp(0) + dp(4)) - (0.5 * cg) * vr * vp
-    new_vz = moved(3)
-    new_t = moved(4) - (courant * 0.4) * temper * diverge
-    return [new_log, new_vr, new_vp, new_vz, new_t]
+    return [
+        lambda: moved(0) - courant * diverge,
+        lambda: moved(1) - courant * (temper * dr(0) + dr(4)) + (0.5 * cg) * vp * vp,
+        lambda: moved(2) - cg * (temper * dp(0) + dp(4)) - (0.5 * cg) * vr * vp,
+        lambda: moved(3),
+        lambda: moved(4) - (courant * 0.4) * temper * diverge,
+    ]
 
 
 def rotate(u, index, lag):
@@ -81,10 +87,13 @@
     n, nr, f_hbm, s_hbm, recv2, f_ref, s_ref, z, send, recv, edge, send2,
     ssem, rsem, esend, erecv, ssem2, rsem2, isem,
 ):
-    f_in = pltpu.make_async_copy(f_hbm, f_ref, isem.at[0])
-    s_in = pltpu.make_async_copy(s_hbm, s_ref, isem.at[1])
-    f_in.start()
-    s_in.start()
+    loads = [
+        pltpu.make_async_copy(f_hbm.at[fs], f_ref.at[fs], isem.at[p])
+        for p, fs in enumerate(PAIRS)
+    ]
+    loads.append(pltpu.make_async_copy(s_hbm, s_ref, isem.at[len(PAIRS)]))
+    for load in loads:
+        load.start()
     r = lax.axis_index("rad")
     t = lax.axis_index("azi")
     tiles = f_ref.shape[3] // SUB
@@ -110,31 +119,6 @@
     lane = lax.broadcasted_iota(jnp.int32, (SUB, LANES), 1)
     low = lane < HALF
 
-    s_in.wait()
-    f_in.wait()
-    shifts = s_ref[...].astype(jnp.float32)
-    rest = jnp.zeros((HALF - STEPS, LANES), jnp.float32)
-    stacks = [
-        f_ref[0:2, 0].reshape(LANES, LANES),
-        f_ref[2:4, 0].reshape(LANES, LANES),
-        jnp.concatenate([f_ref[4, 0], shifts, rest], axis=0),
-    ]
-    for p, stack in enumerate(stacks):
-        z[:, p] = stack.T.reshape(tiles, SUB, LANES)
-
-    for k in range(n):
-        a, b = 2 * k, 2 * k + 1
-        for p in range(2):
-            send[k, 2 * p] = z[a, p]
-            send[k, 2 * p + 1] = z[b, p]
-        send[k, 4] = jnp.where(low, z[a, 2], pltpu.roll(z[b, 2], HALF, 1))
-        above, below = max(a - 1, 0), min(b + 1, tiles - 1)
-        for p in range(3):
-            send[k, 5 + p] = jnp.where(sub >= SUB - STEPS, z[above, p], z[below, p])
-
-    needed = n - 1 + (r > 0).astype(jnp.int32) + (r < nr - 1).astype(jnp.int32)
-    pl.semaphore_wait(barrier, needed)
-
     def edge_copy(which, row, slot, device):
         return pltpu.make_async_remote_copy(
             src_ref=z.at[row], dst_ref=edge.at[slot], send_sem=esend.at[which],
@@ -144,22 +128,48 @@
     to_inner = edge_copy(0, 0, t, {"rad": r - 1, "azi": n - 1})
     to_outer = edge_copy(1, tiles - 1, t, {"rad": r + 1, "azi": 0})
 
-    @pl.when(r > 0)
-    def _():
-        to_inner.start()
-
-    @pl.when(r < nr - 1)
-    def _():
-        to_outer.start()
-
     copies = []
-    for d, peer in enumerate(peers):
-        copy = pltpu.make_async_remote_copy(
-            src_ref=send.at[peer], dst_ref=recv.at[t], send_sem=ssem.at[d],
-            recv_sem=rsem.at[d], device_id={"azi": peer},
-        )
-        copy.start()
-        copies.append(copy)
+    for p, fs in enumerate(PAIRS):
+        loads[p].wait()
+        if p < 2:
+            stack = f_ref[fs, 0].reshape(LANES, LANES)
+        else:
+            loads[3].wait()
+            shifts = s_ref[...].astype(jnp.float32)
+            rest = jnp.zeros((HALF - STEPS, LANES), jnp.float32)
+            stack = jnp.concatenate([f_ref[4, 0], shifts, rest], axis=0)
+        z[:, p] = stack.T.reshape(tiles, SUB, LANES)
+        for k in range(n):
+            a, b = 2 * k, 2 * k + 1
+            if p < 2:
+                send[k, 3 * p] = z[a, p]
+                send[k, 3 * p + 1] = z[b, p]
+            else:
+                send[k, 6] = jnp.where(low, z[a, p], pltpu.roll(z[b, p], HALF, 1))
+            above, below = max(a - 1, 0), min(b + 1, tiles - 1)
+            halo = jnp.where(sub >= SUB - STEPS, z[above, p], z[below, p])
+            send[k, THERE[p].stop - 1] = halo
+
+        if p == 0:
+            needed = n - 1 + (r > 0).astype(jnp.int32) + (r < nr - 1).astype(jnp.int32)
+            pl.semaphore_wait(barrier, needed)
+        if p == 2:
+
+            @pl.when(r > 0)
+            def _():
+                to_inner.start()
+
+            @pl.when(r < nr - 1)
+            def _():
+                to_outer.start()
+
+        for d, peer in enumerate(peers):
+            copy = pltpu.make_async_remote_copy(
+                src_ref=send.at[peer, THERE[p]], dst_ref=recv.at[t, THERE[p]],
+                send_sem=ssem.at[p, d], recv_sem=rsem.at[p, d], device_id={"azi": peer},
+            )
+            copy.start()
+            copies.append(copy)
     recv[t] = send[t]
 
     rows = 3 * SUB
@@ -183,7 +193,8 @@
         for b in range(n):
             edge_copy(0, 0, b, {"rad": lax.rem(r + 1, nr), "azi": 0}).wait_recv()
             for p in range(3):
-                recv[b, 5 + p] = jnp.where(take, edge[b, p], recv[b, 5 + p])
+                at = THERE[p].stop - 1
+                recv[b, at] = jnp.where(take, edge[b, p], recv[b, at])
 
     fields = [[] for _ in range(FIELDS)]
     for q in range(n // 2):
@@ -191,9 +202,9 @@
         for p in range(2):
             for h in range(2):
                 fields[2 * p + h].append(
-                    jnp.concatenate([got[2 * p][h], got[2 * p + 1][h], got[5 + p][h]], axis=0)
+                    jnp.concatenate([got[3 * p + i][h] for i in range(3)], axis=0)
                 )
-        fields[4].append(jnp.concatenate([got[4][0], got[4][1], got[7][0]], axis=0))
+        fields[4].append(jnp.concatenate([got[6][0], got[6][1], got[7][0]], axis=0))
     fields = [jnp.where(inside, jnp.concatenate(u, axis=1), 0.0) for u in fields]
 
     carried = jnp.concatenate([z[2 * t, 2], z[2 * t + 1, 2], recv[0, 7]], axis=0)
@@ -205,29 +216,34 @@
         part = shift - whole * LANES
         index = jnp.bitwise_and(lanes - part, LANES - 1)
         lag = whole + jnp.where(lanes < part, 1, 0)
-        fields = [jnp.where(inside, u, 0.0) for u in step_update(fields, inverse)]
-        fields = [rotate(u, index, lag) for u in fields]
-
-    for q in range(n // 2):
-        f = [u[:, q * LANES : (q + 1) * LANES] for u in fields]
-        for p in range(2):
-            for i in range(2):
-                rs = slice(i * SUB, (i + 1) * SUB)
-                even, odd = halves(f[2 * p][rs], f[2 * p + 1][rs], low)
-                send2[2 * q, 2 * p + i] = even
-                send2[2 * q + 1, 2 * p + i] = odd
-        even, odd = halves(f[4][:SUB], f[4][SUB : 2 * SUB], low)
-        send2[2 * q, 4] = even
-        send2[2 * q + 1, 4] = odd
-
+        if step < STEPS - 1:
+            fields = [jnp.where(inside, new(), 0.0) for new in updates(fields, inverse, rows)]
+            fields = [rotate(u, index, lag) for u in fields]
+
+    own = 2 * SUB
+    news = updates(fields, inverse, own)
     backs = []
-    for d, peer in enumerate(peers):
-        copy = pltpu.make_async_remote_copy(
-            src_ref=send2.at[peer], dst_ref=recv2.at[t], send_sem=ssem2.at[d],
-            recv_sem=rsem2.at[d], device_id={"azi": peer},
-        )
-        copy.start()
-        backs.append(copy)
+    for p, fs in enumerate(PAIRS):
+        pair = [rotate(new(), index[:own], lag[:own]) for new in news[fs]]
+        for q in range(n // 2):
+            f = [u[:, q * LANES : (q + 1) * LANES] for u in pair]
+            if p < 2:
+                for i in range(2):
+                    rs = slice(i * SUB, (i + 1) * SUB)
+                    even, odd = halves(f[0][rs], f[1][rs], low)
+                    send2[2 * q, 2 * p + i] = even
+                    send2[2 * q + 1, 2 * p + i] = odd
+            else:
+                even, odd = halves(f[0][:SUB], f[0][SUB:], low)
+                send2[2 * q, 4] = even
+                send2[2 * q + 1, 4] = odd
+        for d, peer in enumerate(peers):
+            copy = pltpu.make_async_remote_copy(
+                src_ref=send2.at[peer, BACK[p]], dst_ref=recv2.at[t, BACK[p]],
+                send_sem=ssem2.at[p, d], recv_sem=rsem2.at[p, d], device_id={"azi": peer},
+            )
+            copy.start()
+            backs.append(copy)
     recv2[t] = send2[t]
 
     for copy in copies:
@@ -286,13 +302,13 @@
             pltpu.VMEM((n, 8) + tile, jnp.float32),
             pltpu.VMEM((n, 3) + tile, jnp.float32),
             pltpu.VMEM((n, 5) + tile, jnp.float32),
-            dma((n - 1,)),
-            dma((n - 1,)),
+            dma((3, n - 1)),
+            dma((3, n - 1)),
             dma((2,)),
             dma((n,)),
-            dma((n - 1,)),
-            dma((n - 1,)),
-            dma((2,)),
+            dma((3, n - 1)),
+            dma((3, n - 1)),
+            dma((4,)),
         ],
         compiler_params=pltpu.CompilerParams(
             collective_id=0, has_side_effects=True, vmem_limit_bytes=16 * 1024 * 1024

time: 15.1 us -> 16.6 us (1.099)
  Pallas kernels: 14.9 us -> 16.4 us
    pallas_call x1, Pallas kernels: 14.1 us -> 15.6 us  [by_cycles(): pl.pallas_call(functools.partial(kernel, n, nr), out_shape=pltpu.VMEM((n,...]
where the time goes in v4:
time: 16.6 us; the launch traced here: 16.4 us
  Pallas kernels  16.4 us (99%)
    pallas_call x1, Pallas kernels, by_cycles(): pl.pallas_call(functools.partial(kernel, n, nr), out_shape=pltpu.VMEM((n,...  15.6 us
    pallas_call x1, Pallas kernels, by_cycles(): pl.pallas_call(to_cells, out_shape=jax.ShapeDtypeStruct(fields.shape, fie...  0.8 us

profile of v4, /device:TPU:0, one launch (start us, length us, event | category | flops | bytes accessed | tf_op | source)
XLA Modules:
  0.0 16.4 jit_solution(5317788981675698684)
XLA Ops:
  0.0 15.6 %shard_map.28.got = f32[8,5,8,128]{3,2,1,0:T(8,128)S(1)} custom-call(f32[5,1,64,128]{3,2,1,0:T(8,128)} %f_hbm.1, s32[3,128]{1,0:T(4,128)} %s_hbm.1), custom_call_target="tpu_custom_call" | custom-call | tf_op jit(solution)/shard_map/pallas_call | solution.py:292
  15.6 0.8 %shard_map.29 = f32[5,1,64,128]{3,2,1,0:T(8,128)} custom-call(f32[8,5,8,128]{3,2,1,0:T(8,128)S(1)} %shard_map.28.got), custom_call_target="tpu_custom_call" | custom-call | tf_op jit(solution)/shard_map/pallas_call | solution.py:320

commit v5 on v4

--- a/solution.py
+++ b/solution.py
@@ -15,7 +15,6 @@
 HALF = 64
 PAIRS = (slice(0, 2), slice(2, 4), slice(4, 5))
 THERE = (slice(0, 3), slice(3, 6), slice(6, 8))
-BACK = (slice(0, 2), slice(2, 4), slice(4, 5))
 
 courant = 0.2
 viscous = 0.1
@@ -88,10 +87,9 @@
     ssem, rsem, esend, erecv, ssem2, rsem2, isem,
 ):
     loads = [
-        pltpu.make_async_copy(f_hbm.at[fs], f_ref.at[fs], isem.at[p])
-        for p, fs in enumerate(PAIRS)
+        pltpu.make_async_copy(f_hbm, f_ref, isem.at[0]),
+        pltpu.make_async_copy(s_hbm, s_ref, isem.at[1]),
     ]
-    loads.append(pltpu.make_async_copy(s_hbm, s_ref, isem.at[len(PAIRS)]))
     for load in loads:
         load.start()
     r = lax.axis_index("rad")
@@ -122,19 +120,18 @@
     def edge_copy(which, row, slot, device):
         return pltpu.make_async_remote_copy(
             src_ref=z.at[row], dst_ref=edge.at[slot], send_sem=esend.at[which],
-            recv_sem=erecv.at[slot], device_id=device,
+            recv_sem=erecv, device_id=device,
         )
 
     to_inner = edge_copy(0, 0, t, {"rad": r - 1, "azi": n - 1})
     to_outer = edge_copy(1, tiles - 1, t, {"rad": r + 1, "azi": 0})
 
-    copies = []
+    for load in loads:
+        load.wait()
     for p, fs in enumerate(PAIRS):
-        loads[p].wait()
         if p < 2:
             stack = f_ref[fs, 0].reshape(LANES, LANES)
         else:
-            loads[3].wait()
             shifts = s_ref[...].astype(jnp.float32)
             rest = jnp.zeros((HALF - STEPS, LANES), jnp.float32)
             stack = jnp.concatenate([f_ref[4, 0], shifts, rest], axis=0)
@@ -150,26 +147,26 @@
             halo = jnp.where(sub >= SUB - STEPS, z[above, p], z[below, p])
             send[k, THERE[p].stop - 1] = halo
 
-        if p == 0:
-            needed = n - 1 + (r > 0).astype(jnp.int32) + (r < nr - 1).astype(jnp.int32)
-            pl.semaphore_wait(barrier, needed)
-        if p == 2:
-
-            @pl.when(r > 0)
-            def _():
-                to_inner.start()
-
-            @pl.when(r < nr - 1)
-            def _():
-                to_outer.start()
-
-        for d, peer in enumerate(peers):
-            copy = pltpu.make_async_remote_copy(
-                src_ref=send.at[peer, THERE[p]], dst_ref=recv.at[t, THERE[p]],
-                send_sem=ssem.at[p, d], recv_sem=rsem.at[p, d], device_id={"azi": peer},
-            )
-            copy.start()
-            copies.append(copy)
+    needed = n - 1 + (r > 0).astype(jnp.int32) + (r < nr - 1).astype(jnp.int32)
+    pl.semaphore_wait(barrier, needed)
+
+    @pl.when(r > 0)
+    def _():
+        to_inner.start()
+
+    @pl.when(r < nr - 1)
+    def _():
+        to_outer.start()
+
+    def to_peer(src, dst, send_sem, recv_sem, peer):
+        return pltpu.make_async_remote_copy(
+            src_ref=src, dst_ref=dst, send_sem=send_sem, recv_sem=recv_sem,
+            device_id={"azi": peer},
+        )
+
+    for peer in peers:
+        to_peer(send.at[peer], recv.at[t], ssem, rsem, peer).start()
+    there = to_peer(send.at[1:], recv.at[1:], ssem, rsem, peers[0])
     recv[t] = send[t]
 
     rows = 3 * SUB
@@ -182,16 +179,18 @@
     radius = 1.0 + (row.astype(jnp.float32) + 0.5) / jnp.float32(total)
     inverse = 1.0 / radius
 
-    for copy in copies:
-        copy.wait_recv()
+    there.wait_recv()
 
     @pl.when(top_edge | bottom_edge)
     def _():
         first = jnp.where(t == 0, SUB - STEPS, 0)
         last = jnp.where(t == 0, SUB, STEPS)
         take = (sub >= first) & (sub < last)
+        pltpu.make_async_remote_copy(
+            src_ref=z.at[:n], dst_ref=edge, send_sem=esend.at[0], recv_sem=erecv,
+            device_id={"rad": lax.rem(r + 1, nr)},
+        ).wait_recv()
         for b in range(n):
-            edge_copy(0, 0, b, {"rad": lax.rem(r + 1, nr), "azi": 0}).wait_recv()
             for p in range(3):
                 at = THERE[p].stop - 1
                 recv[b, at] = jnp.where(take, edge[b, p], recv[b, at])
@@ -222,7 +221,6 @@
 
     own = 2 * SUB
     news = updates(fields, inverse, own)
-    backs = []
     for p, fs in enumerate(PAIRS):
         pair = [rotate(new(), index[:own], lag[:own]) for new in news[fs]]
         for q in range(n // 2):
@@ -237,17 +235,12 @@
                 even, odd = halves(f[0][:SUB], f[0][SUB:], low)
                 send2[2 * q, 4] = even
                 send2[2 * q + 1, 4] = odd
-        for d, peer in enumerate(peers):
-            copy = pltpu.make_async_remote_copy(
-                src_ref=send2.at[peer, BACK[p]], dst_ref=recv2.at[t, BACK[p]],
-                send_sem=ssem2.at[p, d], recv_sem=rsem2.at[p, d], device_id={"azi": peer},
-            )
-            copy.start()
-            backs.append(copy)
+    for peer in peers:
+        to_peer(send2.at[peer], recv2.at[t], ssem2, rsem2, peer).start()
+    back = to_peer(send2.at[1:], recv2.at[1:], ssem2, rsem2, peers[0])
     recv2[t] = send2[t]
 
-    for copy in copies:
-        copy.wait_send()
+    there.wait_send()
 
     @pl.when(r > 0)
     def _():
@@ -257,11 +250,9 @@
     def _():
         to_outer.wait_send()
 
-    for copy in backs:
-        copy.wait_recv()
-
-    for copy in backs:
-        copy.wait_send()
+    back.wait_recv()
+
+    back.wait_send()
 
 
 def to_cells(got, o_hbm, out, sem):
@@ -302,13 +293,13 @@
             pltpu.VMEM((n, 8) + tile, jnp.float32),
             pltpu.VMEM((n, 3) + tile, jnp.float32),
             pltpu.VMEM((n, 5) + tile, jnp.float32),
-            dma((3, n - 1)),
-            dma((3, n - 1)),
+            dma,
+            dma,
             dma((2,)),
-            dma((n,)),
-            dma((3, n - 1)),
-            dma((3, n - 1)),
-            dma((4,)),
+            dma,
+            dma,
+            dma,
+            dma((2,)),
         ],
         compiler_params=pltpu.CompilerParams(
             collective_id=0, has_side_effects=True, vmem_limit_bytes=16 * 1024 * 1024

time: 16.6 us -> 14.8 us (0.89)
  Pallas kernels: 16.4 us -> 14.7 us
    pallas_call x1, Pallas kernels: 15.6 us -> 13.8 us  [by_cycles(): pl.pallas_call(functools.partial(kernel, n, nr), out_shape=pltpu.VMEM((n,...]
where the time goes in v5:
time: 14.8 us; the launch traced here: 14.7 us
  Pallas kernels  14.7 us (99%)
    pallas_call x1, Pallas kernels, by_cycles(): pl.pallas_call(functools.partial(kernel, n, nr), out_shape=pltpu.VMEM((n,...  13.8 us
    pallas_call x1, Pallas kernels, by_cycles(): pl.pallas_call(to_cells, out_shape=jax.ShapeDtypeStruct(fields.shape, fie...  0.8 us

profile of v5, /device:TPU:0, one launch (start us, length us, event | category | flops | bytes accessed | tf_op | source)
XLA Modules:
  0.0 14.7 jit_solution(16203393697781572587)
XLA Ops:
  0.0 13.8 %shard_map.28.got = f32[8,5,8,128]{3,2,1,0:T(8,128)S(1)} custom-call(f32[5,1,64,128]{3,2,1,0:T(8,128)} %f_hbm.1, s32[3,128]{1,0:T(4,128)} %s_hbm.1), custom_call_target="tpu_custom_call" | custom-call | tf_op jit(solution)/shard_map/pallas_call | solution.py:283
  13.9 0.8 %shard_map.29 = f32[5,1,64,128]{3,2,1,0:T(8,128)} custom-call(f32[8,5,8,128]{3,2,1,0:T(8,128)S(1)} %shard_map.28.got), custom_call_target="tpu_custom_call" | custom-call | tf_op jit(solution)/shard_map/pallas_call | solution.py:311

commit v6 on v5

--- a/solution.py
+++ b/solution.py
@@ -14,7 +14,6 @@
 SUB = 8
 HALF = 64
 PAIRS = (slice(0, 2), slice(2, 4), slice(4, 5))
-THERE = (slice(0, 3), slice(3, 6), slice(6, 8))
 
 courant = 0.2
 viscous = 0.1
@@ -83,7 +82,7 @@
 
 
 def kernel(
-    n, nr, f_hbm, s_hbm, recv2, f_ref, s_ref, z, send, recv, edge, send2,
+    n, nr, f_hbm, s_hbm, recv2, f_ref, s_ref, z, send, recv, halo, eout, edge, send2,
     ssem, rsem, esend, erecv, ssem2, rsem2, isem,
 ):
     loads = [
@@ -95,7 +94,10 @@
     r = lax.axis_index("rad")
     t = lax.axis_index("azi")
     tiles = f_ref.shape[3] // SUB
-    peers = [lax.rem(t + d, n) for d in range(1, n)]
+    chip, core = lax.div(t, 2), lax.rem(t, 2)
+    chips = n // 2
+    far = [chips - 1 - chip, lax.rem(chip + 2, chips), chip + 1 - 2 * lax.rem(chip, 2)]
+    peers = [2 * c + h for c in far for h in (core, 1 - core)] + [2 * chip + 1 - core]
     top_edge = (t == 0) & (r > 0)
     bottom_edge = (t == n - 1) & (r < nr - 1)
 
@@ -117,14 +119,14 @@
     lane = lax.broadcasted_iota(jnp.int32, (SUB, LANES), 1)
     low = lane < HALF
 
-    def edge_copy(which, row, slot, device):
+    def edge_copy(which, slot, device):
         return pltpu.make_async_remote_copy(
-            src_ref=z.at[row], dst_ref=edge.at[slot], send_sem=esend.at[which],
+            src_ref=eout.at[which], dst_ref=edge.at[slot], send_sem=esend.at[which],
             recv_sem=erecv, device_id=device,
         )
 
-    to_inner = edge_copy(0, 0, t, {"rad": r - 1, "azi": n - 1})
-    to_outer = edge_copy(1, tiles - 1, t, {"rad": r + 1, "azi": 0})
+    to_inner = edge_copy(0, t, {"rad": r - 1, "azi": n - 1})
+    to_outer = edge_copy(1, t, {"rad": r + 1, "azi": 0})
 
     for load in loads:
         load.wait()
@@ -136,16 +138,25 @@
             rest = jnp.zeros((HALF - STEPS, LANES), jnp.float32)
             stack = jnp.concatenate([f_ref[4, 0], shifts, rest], axis=0)
         z[:, p] = stack.T.reshape(tiles, SUB, LANES)
-        for k in range(n):
-            a, b = 2 * k, 2 * k + 1
-            if p < 2:
-                send[k, 3 * p] = z[a, p]
-                send[k, 3 * p + 1] = z[b, p]
-            else:
-                send[k, 6] = jnp.where(low, z[a, p], pltpu.roll(z[b, p], HALF, 1))
-            above, below = max(a - 1, 0), min(b + 1, tiles - 1)
-            halo = jnp.where(sub >= SUB - STEPS, z[above, p], z[below, p])
-            send[k, THERE[p].stop - 1] = halo
+
+    def halo_tile(p, k):
+        above, below = jnp.maximum(2 * k - 1, 0), jnp.minimum(2 * k + 2, tiles - 1)
+        return jnp.where(sub >= SUB - STEPS, z[above, p], z[below, p])
+
+    for k in range(n):
+        a, b = 2 * k, 2 * k + 1
+        for p in range(2):
+            send[k, 2 * p] = z[a, p]
+            send[k, 2 * p + 1] = z[b, p]
+        send[k, 4] = jnp.where(low, z[a, 2], pltpu.roll(z[b, 2], HALF, 1))
+        last = halo_tile(2, k)
+        free = jnp.where(low, pltpu.roll(last, 3, 0), pltpu.roll(pltpu.roll(last, 6, 0), HALF, 1))
+        send[k, 5] = jnp.where((sub == 3) | (sub == 4), free, halo_tile(0, k))
+        send[k, 6] = jnp.where(sub == 3, pltpu.roll(free, 6, 0), halo_tile(1, k))
+    eout[0, 0] = jnp.where(sub < 4, z[0, 0], pltpu.roll(z[0, 1], 4, 0))
+    eout[1, 0] = jnp.where(sub < 4, pltpu.roll(z[tiles - 1, 1], 4, 0), z[tiles - 1, 0])
+    eout[0, 1] = z[0, 2]
+    eout[1, 1] = z[tiles - 1, 2]
 
     needed = n - 1 + (r > 0).astype(jnp.int32) + (r < nr - 1).astype(jnp.int32)
     pl.semaphore_wait(barrier, needed)
@@ -180,6 +191,11 @@
     inverse = 1.0 / radius
 
     there.wait_recv()
+    own_shifts = halo_tile(2, t)
+    for b in range(n):
+        free = jnp.where(sub == 5, pltpu.roll(recv[b, 6], 2, 0), recv[b, 5])
+        bottom, top = pltpu.roll(free, 5, 0), pltpu.roll(pltpu.roll(free, 2, 0), HALF, 1)
+        halo[b] = jnp.where(low, jnp.where(sub < 4, bottom, top), own_shifts)
 
     @pl.when(top_edge | bottom_edge)
     def _():
@@ -187,26 +203,26 @@
         last = jnp.where(t == 0, SUB, STEPS)
         take = (sub >= first) & (sub < last)
         pltpu.make_async_remote_copy(
-            src_ref=z.at[:n], dst_ref=edge, send_sem=esend.at[0], recv_sem=erecv,
+            src_ref=recv.at[:, :2], dst_ref=edge, send_sem=esend.at[0], recv_sem=erecv,
             device_id={"rad": lax.rem(r + 1, nr)},
         ).wait_recv()
         for b in range(n):
-            for p in range(3):
-                at = THERE[p].stop - 1
-                recv[b, at] = jnp.where(take, edge[b, p], recv[b, at])
+            recv[b, 5] = jnp.where(take, edge[b, 0], recv[b, 5])
+            recv[b, 6] = jnp.where(take, pltpu.roll(edge[b, 0], 4, 0), recv[b, 6])
+            halo[b] = jnp.where(take, edge[b, 1], halo[b])
 
     fields = [[] for _ in range(FIELDS)]
     for q in range(n // 2):
-        got = [halves(recv[2 * q, i], recv[2 * q + 1, i], low) for i in range(8)]
+        got = [halves(recv[2 * q, i], recv[2 * q + 1, i], low) for i in range(7)]
         for p in range(2):
             for h in range(2):
-                fields[2 * p + h].append(
-                    jnp.concatenate([got[3 * p + i][h] for i in range(3)], axis=0)
-                )
-        fields[4].append(jnp.concatenate([got[6][0], got[6][1], got[7][0]], axis=0))
+                tiles_of = (got[2 * p][h], got[2 * p + 1][h], got[5 + p][h])
+                fields[2 * p + h].append(jnp.concatenate(tiles_of, axis=0))
+        last = jnp.where(low, halo[2 * q], pltpu.roll(halo[2 * q + 1], HALF, 1))
+        fields[4].append(jnp.concatenate([got[4][0], got[4][1], last], axis=0))
     fields = [jnp.where(inside, jnp.concatenate(u, axis=1), 0.0) for u in fields]
 
-    carried = jnp.concatenate([z[2 * t, 2], z[2 * t + 1, 2], recv[0, 7]], axis=0)
+    carried = jnp.concatenate([z[2 * t, 2], z[2 * t + 1, 2], halo[0]], axis=0)
     lanes = lax.broadcasted_iota(jnp.int32, (rows, LANES), 1)
     for step in range(STEPS):
         shift = carried[:, HALF + step : HALF + step + 1].astype(jnp.int32)
@@ -289,9 +305,11 @@
             pltpu.VMEM(fields.shape, fields.dtype),
             pltpu.VMEM(shifts.shape, shifts.dtype),
             pltpu.VMEM((tiles, 3) + tile, jnp.float32),
-            pltpu.VMEM((n, 8) + tile, jnp.float32),
-            pltpu.VMEM((n, 8) + tile, jnp.float32),
-            pltpu.VMEM((n, 3) + tile, jnp.float32),
+            pltpu.VMEM((n, 7) + tile, jnp.float32),
+            pltpu.VMEM((n, 7) + tile, jnp.float32),
+            pltpu.VMEM((n,) + tile, jnp.float32),
+            pltpu.VMEM((2, 2) + tile, jnp.float32),
+            pltpu.VMEM((n, 2) + tile, jnp.float32),
             pltpu.VMEM((n, 5) + tile, jnp.float32),
             dma,
             dma,

time: 14.8 us -> 14.3 us (0.966)
  Pallas kernels: 14.7 us -> 14.2 us
    pallas_call x1, Pallas kernels: 13.8 us -> 13.4 us  [by_cycles(): pl.pallas_call(functools.partial(kernel, n, nr), out_shape=pltpu.VMEM((n,...]
where the time goes in v6:
time: 14.3 us; the launch traced here: 14.2 us
  Pallas kernels  14.2 us (99%)
    pallas_call x1, Pallas kernels, by_cycles(): pl.pallas_call(functools.partial(kernel, n, nr), out_shape=pltpu.VMEM((n,...  13.4 us
    pallas_call x1, Pallas kernels, by_cycles(): pl.pallas_call(to_cells, out_shape=jax.ShapeDtypeStruct(fields.shape, fie...  0.8 us

profile of v6, /device:TPU:0, one launch (start us, length us, event | category | flops | bytes accessed | tf_op | source)
XLA Modules:
  0.0 14.2 jit_solution(5503730266613376139)
XLA Ops:
  0.0 13.4 %shard_map.28.got = f32[8,5,8,128]{3,2,1,0:T(8,128)S(1)} custom-call(f32[5,1,64,128]{3,2,1,0:T(8,128)} %f_hbm.1, s32[3,128]{1,0:T(4,128)} %s_hbm.1), custom_call_target="tpu_custom_call" | custom-call | tf_op jit(solution)/shard_map/pallas_call | solution.py:299
  13.4 0.8 %shard_map.29 = f32[5,1,64,128]{3,2,1,0:T(8,128)} custom-call(f32[8,5,8,128]{3,2,1,0:T(8,128)S(1)} %shard_map.28.got), custom_call_target="tpu_custom_call" | custom-call | tf_op jit(solution)/shard_map/pallas_call | solution.py:329

commit v7 on v6

--- a/solution.py
+++ b/solution.py
@@ -33,36 +33,44 @@
     behind = [pltpu.roll(u, 1, 1) for u in f]
     ahead = [pltpu.roll(u, u.shape[1] - 1, 1) for u in f]
     _, vr, vp, _, temper = f
-    r_pos = courant * jnp.maximum(vr, 0.0)
-    r_neg = courant * jnp.minimum(vr, 0.0)
     cg = courant * inverse
-    p_pos = cg * jnp.maximum(vp, 0.0)
-    p_neg = cg * jnp.minimum(vp, 0.0)
     vg2 = viscous * inverse * inverse
+    into, out = courant * jnp.maximum(vr, 0.0), -courant * jnp.minimum(vr, 0.0)
+    back, fwd = cg * jnp.maximum(vp, 0.0), -cg * jnp.minimum(vp, 0.0)
+    w_in, w_out, w_back, w_fwd = into + viscous, out + viscous, back + vg2, fwd + vg2
 
     def moved(i):
         u = f[i]
-        d_in, d_out = u - inner[i], outer[i] - u
-        d_back, d_fwd = u - behind[i], ahead[i] - u
-        base = u - (r_pos * d_in + r_neg * d_out + p_pos * d_back + p_neg * d_fwd)
-        if i == 0:
-            return base
         polar = (u + u) - 2.0 * u
-        return base + (viscous * ((d_out - d_in) + polar) + vg2 * (d_fwd - d_back))
+        return (
+            u + viscous * polar
+            + (w_out * (outer[i] - u) - w_in * (u - inner[i]))
+            + (w_fwd * (ahead[i] - u) - w_back * (u - behind[i]))
+        )
+
+    def advected(i):
+        u = f[i]
+        return (
+            u
+            + (out * (outer[i] - u) - into * (u - inner[i]))
+            + (fwd * (ahead[i] - u) - back * (u - behind[i]))
+        )
 
     def dr(i):
-        return (outer[i] - inner[i]) * 0.5
+        return outer[i] - inner[i]
 
     def dp(i):
-        return (ahead[i] - behind[i]) * 0.5
-
+        return ahead[i] - behind[i]
+
+    half = 0.5 * courant
+    half_g = 0.5 * cg
     diverge = dr(1) + inverse * dp(2)
     return [
-        lambda: moved(0) - courant * diverge,
-        lambda: moved(1) - courant * (temper * dr(0) + dr(4)) + (0.5 * cg) * vp * vp,
-        lambda: moved(2) - cg * (temper * dp(0) + dp(4)) - (0.5 * cg) * vr * vp,
+        lambda: advected(0) - half * diverge,
+        lambda: moved(1) - half * (temper * dr(0) + dr(4)) + half_g * vp * vp,
+        lambda: moved(2) - half_g * (temper * dp(0) + dp(4) + vr * vp),
         lambda: moved(3),
-        lambda: moved(4) - (courant * 0.4) * temper * diverge,
+        lambda: moved(4) - (0.4 * half) * temper * diverge,
     ]
 
 
@@ -86,9 +94,10 @@
     ssem, rsem, esend, erecv, ssem2, rsem2, isem,
 ):
     loads = [
-        pltpu.make_async_copy(f_hbm, f_ref, isem.at[0]),
-        pltpu.make_async_copy(s_hbm, s_ref, isem.at[1]),
+        pltpu.make_async_copy(f_hbm.at[fs], f_ref.at[fs], isem.at[p])
+        for p, fs in enumerate(PAIRS)
     ]
+    loads.append(pltpu.make_async_copy(s_hbm, s_ref, isem.at[3]))
     for load in loads:
         load.start()
     r = lax.axis_index("rad")
@@ -128,12 +137,12 @@
     to_inner = edge_copy(0, t, {"rad": r - 1, "azi": n - 1})
     to_outer = edge_copy(1, t, {"rad": r + 1, "azi": 0})
 
-    for load in loads:
-        load.wait()
     for p, fs in enumerate(PAIRS):
+        loads[p].wait()
         if p < 2:
             stack = f_ref[fs, 0].reshape(LANES, LANES)
         else:
+            loads[3].wait()
             shifts = s_ref[...].astype(jnp.float32)
             rest = jnp.zeros((HALF - STEPS, LANES), jnp.float32)
             stack = jnp.concatenate([f_ref[4, 0], shifts, rest], axis=0)
@@ -190,6 +199,11 @@
     radius = 1.0 + (row.astype(jnp.float32) + 0.5) / jnp.float32(total)
     inverse = 1.0 / radius
 
+    own = 2 * SUB
+
+    def inner_rows(u):
+        return jnp.concatenate([u[:own], jnp.where(inside[own:], u[own:], 0.0)], axis=0)
+
     there.wait_recv()
     own_shifts = halo_tile(2, t)
     for b in range(n):
@@ -220,7 +234,7 @@
                 fields[2 * p + h].append(jnp.concatenate(tiles_of, axis=0))
         last = jnp.where(low, halo[2 * q], pltpu.roll(halo[2 * q + 1], HALF, 1))
         fields[4].append(jnp.concatenate([got[4][0], got[4][1], last], axis=0))
-    fields = [jnp.where(inside, jnp.concatenate(u, axis=1), 0.0) for u in fields]
+    fields = [inner_rows(jnp.concatenate(u, axis=1)) for u in fields]
 
     carried = jnp.concatenate([z[2 * t, 2], z[2 * t + 1, 2], halo[0]], axis=0)
     lanes = lax.broadcasted_iota(jnp.int32, (rows, LANES), 1)
@@ -232,10 +246,9 @@
         index = jnp.bitwise_and(lanes - part, LANES - 1)
         lag = whole + jnp.where(lanes < part, 1, 0)
         if step < STEPS - 1:
-            fields = [jnp.where(inside, new(), 0.0) for new in updates(fields, inverse, rows)]
+            fields = [inner_rows(new()) for new in updates(fields, inverse, rows)]
             fields = [rotate(u, index, lag) for u in fields]
 
-    own = 2 * SUB
     news = updates(fields, inverse, own)
     for p, fs in enumerate(PAIRS):
         pair = [rotate(new(), index[:own], lag[:own]) for new in news[fs]]
@@ -317,7 +330,7 @@
             dma,
             dma,
             dma,
-            dma((2,)),
+            dma((4,)),
         ],
         compiler_params=pltpu.CompilerParams(
             collective_id=0, has_side_effects=True, vmem_limit_bytes=16 * 1024 * 1024

time: 14.3 us -> 14.3 us (level)
  no operation moved by 1% of the time
where the time goes in v7:
time: 14.3 us; the launch traced here: 14.2 us
  Pallas kernels  14.2 us (99%)
    pallas_call x1, Pallas kernels, by_cycles(): pl.pallas_call(functools.partial(kernel, n, nr), out_shape=pltpu.VMEM((n,...  13.4 us
    pallas_call x1, Pallas kernels, by_cycles(): pl.pallas_call(to_cells, out_shape=jax.ShapeDtypeStruct(fields.shape, fie...  0.8 us

profile of v7, /device:TPU:0, one launch (start us, length us, event | category | flops | bytes accessed | tf_op | source)
XLA Modules:
  0.0 14.2 jit_solution(17754022423292671832)
XLA Ops:
  0.0 13.4 %shard_map.28.got = f32[8,5,8,128]{3,2,1,0:T(8,128)S(1)} custom-call(f32[5,1,64,128]{3,2,1,0:T(8,128)} %f_hbm.1, s32[3,128]{1,0:T(4,128)} %s_hbm.1), custom_call_target="tpu_custom_call" | custom-call | tf_op jit(solution)/shard_map/pallas_call | solution.py:312
  13.4 0.8 %shard_map.29 = f32[5,1,64,128]{3,2,1,0:T(8,128)} custom-call(f32[8,5,8,128]{3,2,1,0:T(8,128)S(1)} %shard_map.28.got), custom_call_target="tpu_custom_call" | custom-call | tf_op jit(solution)/shard_map/pallas_call | solution.py:342

commit v8 on v7

--- a/solution.py
+++ b/solution.py
@@ -94,10 +94,9 @@
     ssem, rsem, esend, erecv, ssem2, rsem2, isem,
 ):
     loads = [
-        pltpu.make_async_copy(f_hbm.at[fs], f_ref.at[fs], isem.at[p])
-        for p, fs in enumerate(PAIRS)
+        pltpu.make_async_copy(f_hbm, f_ref, isem.at[0]),
+        pltpu.make_async_copy(s_hbm, s_ref, isem.at[1]),
     ]
-    loads.append(pltpu.make_async_copy(s_hbm, s_ref, isem.at[3]))
     for load in loads:
         load.start()
     r = lax.axis_index("rad")
@@ -105,8 +104,12 @@
     tiles = f_ref.shape[3] // SUB
     chip, core = lax.div(t, 2), lax.rem(t, 2)
     chips = n // 2
-    far = [chips - 1 - chip, lax.rem(chip + 2, chips), chip + 1 - 2 * lax.rem(chip, 2)]
-    peers = [2 * c + h for c in far for h in (core, 1 - core)] + [2 * chip + 1 - core]
+    opposite = chips - 1 - chip
+    beside, across = chip + 1 - 2 * lax.rem(chip, 2), lax.rem(chip + 2, chips)
+    first = jnp.where(core == 0, across, beside)
+    second = jnp.where(core == 0, beside, across)
+    order = [opposite, first, second]
+    peers = [2 * c + h for c in order for h in (core, 1 - core)] + [2 * chip + 1 - core]
     top_edge = (t == 0) & (r > 0)
     bottom_edge = (t == n - 1) & (r < nr - 1)
 
@@ -137,12 +140,12 @@
     to_inner = edge_copy(0, t, {"rad": r - 1, "azi": n - 1})
     to_outer = edge_copy(1, t, {"rad": r + 1, "azi": 0})
 
+    for load in loads:
+        load.wait()
     for p, fs in enumerate(PAIRS):
-        loads[p].wait()
         if p < 2:
             stack = f_ref[fs, 0].reshape(LANES, LANES)
         else:
-            loads[3].wait()
             shifts = s_ref[...].astype(jnp.float32)
             rest = jnp.zeros((HALF - STEPS, LANES), jnp.float32)
             stack = jnp.concatenate([f_ref[4, 0], shifts, rest], axis=0)
@@ -330,7 +333,7 @@
             dma,
             dma,
             dma,
-            dma((4,)),
+            dma((2,)),
         ],
         compiler_params=pltpu.CompilerParams(
             collective_id=0, has_side_effects=True, vmem_limit_bytes=16 * 1024 * 1024

time: 14.3 us -> 14.3 us (level)
  no operation moved by 1% of the time
where the time goes in v8:
time: 14.3 us; the launch traced here: 14.2 us
  Pallas kernels  14.2 us (99%)
    pallas_call x1, Pallas kernels, by_cycles(): pl.pallas_call(functools.partial(kernel, n, nr), out_shape=pltpu.VMEM((n,...  13.4 us
    pallas_call x1, Pallas kernels, by_cycles(): pl.pallas_call(to_cells, out_shape=jax.ShapeDtypeStruct(fields.shape, fie...  0.8 us

profile of v8, /device:TPU:0, one launch (start us, length us, event | category | flops | bytes accessed | tf_op | source)
XLA Modules:
  0.0 14.2 jit_solution(11140384273152906467)
XLA Ops:
  0.0 13.4 %shard_map.28.got = f32[8,5,8,128]{3,2,1,0:T(8,128)S(1)} custom-call(f32[5,1,64,128]{3,2,1,0:T(8,128)} %f_hbm.1, s32[3,128]{1,0:T(4,128)} %s_hbm.1), custom_call_target="tpu_custom_call" | custom-call | tf_op jit(solution)/shard_map/pallas_call | solution.py:315
  13.4 0.8 %shard_map.29 = f32[5,1,64,128]{3,2,1,0:T(8,128)} custom-call(f32[8,5,8,128]{3,2,1,0:T(8,128)S(1)} %shard_map.28.got), custom_call_target="tpu_custom_call" | custom-call | tf_op jit(solution)/shard_map/pallas_call | solution.py:345

commit v9 on v8

--- a/solution.py
+++ b/solution.py
@@ -155,7 +155,7 @@
         above, below = jnp.maximum(2 * k - 1, 0), jnp.minimum(2 * k + 2, tiles - 1)
         return jnp.where(sub >= SUB - STEPS, z[above, p], z[below, p])
 
-    for k in range(n):
+    def build(k):
         a, b = 2 * k, 2 * k + 1
         for p in range(2):
             send[k, 2 * p] = z[a, p]
@@ -165,6 +165,8 @@
         free = jnp.where(low, pltpu.roll(last, 3, 0), pltpu.roll(pltpu.roll(last, 6, 0), HALF, 1))
         send[k, 5] = jnp.where((sub == 3) | (sub == 4), free, halo_tile(0, k))
         send[k, 6] = jnp.where(sub == 3, pltpu.roll(free, 6, 0), halo_tile(1, k))
+
+    build(peers[0])
     eout[0, 0] = jnp.where(sub < 4, z[0, 0], pltpu.roll(z[0, 1], 4, 0))
     eout[1, 0] = jnp.where(sub < 4, pltpu.roll(z[tiles - 1, 1], 4, 0), z[tiles - 1, 0])
     eout[0, 1] = z[0, 2]
@@ -173,22 +175,25 @@
     needed = n - 1 + (r > 0).astype(jnp.int32) + (r < nr - 1).astype(jnp.int32)
     pl.semaphore_wait(barrier, needed)
 
-    @pl.when(r > 0)
-    def _():
-        to_inner.start()
-
-    @pl.when(r < nr - 1)
-    def _():
-        to_outer.start()
-
     def to_peer(src, dst, send_sem, recv_sem, peer):
         return pltpu.make_async_remote_copy(
             src_ref=src, dst_ref=dst, send_sem=send_sem, recv_sem=recv_sem,
             device_id={"azi": peer},
         )
 
-    for peer in peers:
+    for i, peer in enumerate(peers):
         to_peer(send.at[peer], recv.at[t], ssem, rsem, peer).start()
+        build(peers[i + 1] if i < n - 2 else t)
+        if i == 1:
+
+            @pl.when(r > 0)
+            def _():
+                to_inner.start()
+
+            @pl.when(r < nr - 1)
+            def _():
+                to_outer.start()
+
     there = to_peer(send.at[1:], recv.at[1:], ssem, rsem, peers[0])
     recv[t] = send[t]
 
@@ -267,7 +272,8 @@
                 even, odd = halves(f[0][:SUB], f[0][SUB:], low)
                 send2[2 * q, 4] = even
                 send2[2 * q + 1, 4] = odd
-    for peer in peers:
+    others = [jnp.where(j < chip, j, j + 1) for j in range(chips - 1)]
+    for peer in [2 * c + h for c in others for h in (core, 1 - core)] + peers[-1:]:
         to_peer(send2.at[peer], recv2.at[t], ssem2, rsem2, peer).start()
     back = to_peer(send2.at[1:], recv2.at[1:], ssem2, rsem2, peers[0])
     recv2[t] = send2[t]

time: 14.3 us -> 14.1 us (0.986)
  Pallas kernels: 14.2 us -> 13.9 us
    pallas_call x1, Pallas kernels: 13.4 us -> 13.1 us  [by_cycles(): pl.pallas_call(functools.partial(kernel, n, nr), out_shape=pltpu.VMEM((n,...]
where the time goes in v9:
time: 14.1 us; the launch traced here: 14 us
  Pallas kernels  13.9 us (99%)
    pallas_call x1, Pallas kernels, by_cycles(): pl.pallas_call(functools.partial(kernel, n, nr), out_shape=pltpu.VMEM((n,...  13.1 us
    pallas_call x1, Pallas kernels, by_cycles(): pl.pallas_call(to_cells, out_shape=jax.ShapeDtypeStruct(fields.shape, fie...  0.8 us

profile of v9, /device:TPU:0, one launch (start us, length us, event | category | flops | bytes accessed | tf_op | source)
XLA Modules:
  0.0 14.0 jit_solution(77671030707324549)
XLA Ops:
  0.0 13.1 %shard_map.28.got = f32[8,5,8,128]{3,2,1,0:T(8,128)S(1)} custom-call(f32[5,1,64,128]{3,2,1,0:T(8,128)} %f_hbm.1, s32[3,128]{1,0:T(4,128)} %s_hbm.1), custom_call_target="tpu_custom_call" | custom-call | tf_op jit(solution)/shard_map/pallas_call | solution.py:321
  13.2 0.8 %shard_map.29 = f32[5,1,64,128]{3,2,1,0:T(8,128)} custom-call(f32[8,5,8,128]{3,2,1,0:T(8,128)S(1)} %shard_map.28.got), custom_call_target="tpu_custom_call" | custom-call | tf_op jit(solution)/shard_map/pallas_call | solution.py:351

commit v10 on v9

--- a/solution.py
+++ b/solution.py
@@ -25,10 +25,17 @@
     return first, second
 
 
-def updates(f, inverse, rows):
-    inner = [pltpu.roll(u, 1, 0)[:rows] for u in f]
-    outer = [pltpu.roll(u, u.shape[0] - 1, 0)[:rows] for u in f]
-    f = [u[:rows] for u in f]
+def around(ref, f):
+    for i, u in enumerate(f):
+        ref[i, :SUB] = u[2 * SUB :]
+        ref[i, SUB : 4 * SUB] = u
+        ref[i, 4 * SUB :] = u[:SUB]
+
+
+def updates(ref, inverse, rows):
+    inner = [ref[i, SUB - 1 : SUB - 1 + rows] for i in range(FIELDS)]
+    outer = [ref[i, SUB + 1 : SUB + 1 + rows] for i in range(FIELDS)]
+    f = [ref[i, SUB : SUB + rows] for i in range(FIELDS)]
     inverse = inverse[:rows]
     behind = [pltpu.roll(u, 1, 1) for u in f]
     ahead = [pltpu.roll(u, u.shape[1] - 1, 1) for u in f]
@@ -77,7 +84,7 @@
 def rotate(u, index, lag):
     tiles = u.shape[1] // LANES
     g = [
-        jnp.take_along_axis(u[:, q * LANES : (q + 1) * LANES], index, axis=1)
+        jnp.take_along_axis(u[:, q * LANES : (q + 1) * LANES], index, axis=1, mode="promise_in_bounds")
         for q in range(tiles)
     ]
     out = []
@@ -90,7 +97,7 @@
 
 
 def kernel(
-    n, nr, f_hbm, s_hbm, recv2, f_ref, s_ref, z, send, recv, halo, eout, edge, send2,
+    n, nr, f_hbm, s_hbm, recv2, f_ref, s_ref, z, send, recv, halo, eout, edge, send2, ring,
     ssem, rsem, esend, erecv, ssem2, rsem2, isem,
 ):
     loads = [
@@ -254,10 +261,13 @@
         index = jnp.bitwise_and(lanes - part, LANES - 1)
         lag = whole + jnp.where(lanes < part, 1, 0)
         if step < STEPS - 1:
-            fields = [inner_rows(new()) for new in updates(fields, inverse, rows)]
+            around(ring.at[step % 2], fields)
+            news = updates(ring.at[step % 2], inverse, rows)
+            fields = [inner_rows(new()) for new in news]
             fields = [rotate(u, index, lag) for u in fields]
 
-    news = updates(fields, inverse, own)
+    around(ring.at[(STEPS - 1) % 2], fields)
+    news = updates(ring.at[(STEPS - 1) % 2], inverse, own)
     for p, fs in enumerate(PAIRS):
         pair = [rotate(new(), index[:own], lag[:own]) for new in news[fs]]
         for q in range(n // 2):
@@ -333,6 +343,7 @@
             pltpu.VMEM((2, 2) + tile, jnp.float32),
             pltpu.VMEM((n, 2) + tile, jnp.float32),
             pltpu.VMEM((n, 5) + tile, jnp.float32),
+            pltpu.VMEM((2, FIELDS, 5 * SUB, n * HALF), jnp.float32),
             dma,
             dma,
             dma((2,)),

time: 14.1 us -> 14.2 us (level)
  no operation moved by 1% of the time
where the time goes in v10:
time: 14.2 us; the launch traced here: 14 us
  Pallas kernels  14 us (99%)
    pallas_call x1, Pallas kernels, by_cycles(): pl.pallas_call(functools.partial(kernel, n, nr), out_shape=pltpu.VMEM((n,...  13.2 us
    pallas_call x1, Pallas kernels, by_cycles(): pl.pallas_call(to_cells, out_shape=jax.ShapeDtypeStruct(fields.shape, fie...  0.8 us

profile of v10, /device:TPU:0, one launch (start us, length us, event | category | flops | bytes accessed | tf_op | source)
XLA Modules:
  0.0 14.0 jit_solution(6832643095677273241)
XLA Ops:
  0.0 13.2 %shard_map.28.got = f32[8,5,8,128]{3,2,1,0:T(8,128)S(1)} custom-call(f32[5,1,64,128]{3,2,1,0:T(8,128)} %f_hbm.1, s32[3,128]{1,0:T(4,128)} %s_hbm.1), custom_call_target="tpu_custom_call" | custom-call | tf_op jit(solution)/shard_map/pallas_call | solution.py:331
  13.2 0.8 %shard_map.29 = f32[5,1,64,128]{3,2,1,0:T(8,128)} custom-call(f32[8,5,8,128]{3,2,1,0:T(8,128)S(1)} %shard_map.28.got), custom_call_target="tpu_custom_call" | custom-call | tf_op jit(solution)/shard_map/pallas_call | solution.py:362

commit v11 on v9

--- a/solution.py
+++ b/solution.py
@@ -77,7 +77,7 @@
 def rotate(u, index, lag):
     tiles = u.shape[1] // LANES
     g = [
-        jnp.take_along_axis(u[:, q * LANES : (q + 1) * LANES], index, axis=1)
+        jnp.take_along_axis(u[:, q * LANES : (q + 1) * LANES], index, axis=1, mode="promise_in_bounds")
         for q in range(tiles)
     ]
     out = []
@@ -97,8 +97,7 @@
         pltpu.make_async_copy(f_hbm, f_ref, isem.at[0]),
         pltpu.make_async_copy(s_hbm, s_ref, isem.at[1]),
     ]
-    for load in loads:
-        load.start()
+    loads[0].start()
     r = lax.axis_index("rad")
     t = lax.axis_index("azi")
     tiles = f_ref.shape[3] // SUB
@@ -127,6 +126,7 @@
         for b in range(n):
             pl.semaphore_signal(barrier, inc=1, device_id={"rad": r + 1, "azi": b})
 
+    loads[1].start()
     sub = lax.broadcasted_iota(jnp.int32, (SUB, LANES), 0)
     lane = lax.broadcasted_iota(jnp.int32, (SUB, LANES), 1)
     low = lane < HALF
@@ -140,12 +140,12 @@
     to_inner = edge_copy(0, t, {"rad": r - 1, "azi": n - 1})
     to_outer = edge_copy(1, t, {"rad": r + 1, "azi": 0})
 
-    for load in loads:
-        load.wait()
+    loads[0].wait()
     for p, fs in enumerate(PAIRS):
         if p < 2:
             stack = f_ref[fs, 0].reshape(LANES, LANES)
         else:
+            loads[1].wait()
             shifts = s_ref[...].astype(jnp.float32)
             rest = jnp.zeros((HALF - STEPS, LANES), jnp.float32)
             stack = jnp.concatenate([f_ref[4, 0], shifts, rest], axis=0)

time: 14.1 us -> 14.1 us (level)
  no operation moved by 1% of the time
where the time goes in v11:
time: 14.1 us; the launch traced here: 13.9 us
  Pallas kernels  13.9 us (99%)
    pallas_call x1, Pallas kernels, by_cycles(): pl.pallas_call(functools.partial(kernel, n, nr), out_shape=pltpu.VMEM((n,...  13.1 us
    pallas_call x1, Pallas kernels, by_cycles(): pl.pallas_call(to_cells, out_shape=jax.ShapeDtypeStruct(fields.shape, fie...  0.8 us

profile of v11, /device:TPU:0, one launch (start us, length us, event | category | flops | bytes accessed | tf_op | source)
XLA Modules:
  0.0 13.9 jit_solution(412921612852794446)
XLA Ops:
  0.0 13.1 %shard_map.28.got = f32[8,5,8,128]{3,2,1,0:T(8,128)S(1)} custom-call(f32[5,1,64,128]{3,2,1,0:T(8,128)} %f_hbm.1, s32[3,128]{1,0:T(4,128)} %s_hbm.1), custom_call_target="tpu_custom_call" | custom-call | tf_op jit(solution)/shard_map/pallas_call | solution.py:321
  13.1 0.8 %shard_map.29 = f32[5,1,64,128]{3,2,1,0:T(8,128)} custom-call(f32[8,5,8,128]{3,2,1,0:T(8,128)S(1)} %shard_map.28.got), custom_call_target="tpu_custom_call" | custom-call | tf_op jit(solution)/shard_map/pallas_call | solution.py:351

commit v12 on v8

--- a/solution.py
+++ b/solution.py
@@ -267,7 +267,8 @@
                 even, odd = halves(f[0][:SUB], f[0][SUB:], low)
                 send2[2 * q, 4] = even
                 send2[2 * q + 1, 4] = odd
-    for peer in peers:
+    others = [jnp.where(j < chip, j, j + 1) for j in range(chips - 1)]
+    for peer in [2 * c + h for c in others for h in (core, 1 - core)] + peers[-1:]:
         to_peer(send2.at[peer], recv2.at[t], ssem2, rsem2, peer).start()
     back = to_peer(send2.at[1:], recv2.at[1:], ssem2, rsem2, peers[0])
     recv2[t] = send2[t]

time: 14.3 us -> 14.2 us (level)
  Pallas kernels: 14.2 us -> 14 us
where the time goes in v12:
time: 14.2 us; the launch traced here: 14.1 us
  Pallas kernels  14 us (99%)
    pallas_call x1, Pallas kernels, by_cycles(): pl.pallas_call(functools.partial(kernel, n, nr), out_shape=pltpu.VMEM((n,...  13.2 us
    pallas_call x1, Pallas kernels, by_cycles(): pl.pallas_call(to_cells, out_shape=jax.ShapeDtypeStruct(fields.shape, fie...  0.8 us

profile of v12, /device:TPU:0, one launch (start us, length us, event | category | flops | bytes accessed | tf_op | source)
XLA Modules:
  0.0 14.1 jit_solution(4704976413072418357)
XLA Ops:
  0.0 13.2 %shard_map.28.got = f32[8,5,8,128]{3,2,1,0:T(8,128)S(1)} custom-call(f32[5,1,64,128]{3,2,1,0:T(8,128)} %f_hbm.1, s32[3,128]{1,0:T(4,128)} %s_hbm.1), custom_call_target="tpu_custom_call" | custom-call | tf_op jit(solution)/shard_map/pallas_call | solution.py:316
  13.3 0.8 %shard_map.29 = f32[5,1,64,128]{3,2,1,0:T(8,128)} custom-call(f32[8,5,8,128]{3,2,1,0:T(8,128)S(1)} %shard_map.28.got), custom_call_target="tpu_custom_call" | custom-call | tf_op jit(solution)/shard_map/pallas_call | solution.py:346

commit v13 on v9

--- a/solution.py
+++ b/solution.py
@@ -272,8 +272,7 @@
                 even, odd = halves(f[0][:SUB], f[0][SUB:], low)
                 send2[2 * q, 4] = even
                 send2[2 * q + 1, 4] = odd
-    others = [jnp.where(j < chip, j, j + 1) for j in range(chips - 1)]
-    for peer in [2 * c + h for c in others for h in (core, 1 - core)] + peers[-1:]:
+    for peer in peers:
         to_peer(send2.at[peer], recv2.at[t], ssem2, rsem2, peer).start()
     back = to_peer(send2.at[1:], recv2.at[1:], ssem2, rsem2, peers[0])
     recv2[t] = send2[t]

time: 14.1 us -> 14.3 us (1.014)
  Pallas kernels: 13.9 us -> 14.2 us
    pallas_call x1, Pallas kernels: 13.1 us -> 13.4 us  [by_cycles(): pl.pallas_call(functools.partial(kernel, n, nr), out_shape=pltpu.VMEM((n,...]
where the time goes in v13:
time: 14.3 us; the launch traced here: 14.2 us
  Pallas kernels  14.2 us (99%)
    pallas_call x1, Pallas kernels, by_cycles(): pl.pallas_call(functools.partial(kernel, n, nr), out_shape=pltpu.VMEM((n,...  13.4 us
    pallas_call x1, Pallas kernels, by_cycles(): pl.pallas_call(to_cells, out_shape=jax.ShapeDtypeStruct(fields.shape, fie...  0.8 us

profile of v13, /device:TPU:0, one launch (start us, length us, event | category | flops | bytes accessed | tf_op | source)
XLA Modules:
  0.0 14.2 jit_solution(17913714601739905797)
XLA Ops:
  0.0 13.4 %shard_map.28.got = f32[8,5,8,128]{3,2,1,0:T(8,128)S(1)} custom-call(f32[5,1,64,128]{3,2,1,0:T(8,128)} %f_hbm.1, s32[3,128]{1,0:T(4,128)} %s_hbm.1), custom_call_target="tpu_custom_call" | custom-call | tf_op jit(solution)/shard_map/pallas_call | solution.py:320
  13.4 0.8 %shard_map.29 = f32[5,1,64,128]{3,2,1,0:T(8,128)} custom-call(f32[8,5,8,128]{3,2,1,0:T(8,128)S(1)} %shard_map.28.got), custom_call_target="tpu_custom_call" | custom-call | tf_op jit(solution)/shard_map/pallas_call | solution.py:350
